TPU v7x, 32 devices: a whole 2x2x4 slice. The times are simulated.
32 devices in a mesh: frame: 16 (over z, y, core), fsdp: 2 (over x).
Axes of the slice: x: 2, y: 2, z: 4, core: 2. Of those that a mesh axis runs over, the one named last changes fastest.
Arguments:
- frames: bfloat16 [2, 2, 16, 128, 1280], P('fsdp', None, 'frame'), may hold values from -6 to 6
- cotangent: bfloat16 [2, 2, 16, 128, 1280], P('fsdp', None, 'frame'), may hold values from -6 to 6
- block_lengths: int32 [2, 2, 1], P('fsdp'), may hold values from 1 to 16, as said below
- qkv_weight: bfloat16 [3, 1280, 1280], P(None, 'fsdp'), may hold values from -0.15625 to 0.15625
- pair_weight: bfloat16 [2, 1280, 1280], P(None, 'fsdp'), may hold values from -0.15625 to 0.15625
- attn_out_weight: bfloat16 [1280, 1280], P('fsdp'), may hold values from -0.3125 to 0.3125
- ff_up_weight: bfloat16 [1280, 5120], P('fsdp'), may hold values from -0.15625 to 0.15625
- ff_down_weight: bfloat16 [5120, 1280], P('fsdp'), may hold values from -0.15625 to 0.15625
- norm_gains: float32 [3, 1280], replicated, may hold values from 0.1 to 1.9
- biases: float32 [7, 1280], replicated, may hold values from -3 to 3
- up_bias: float32 [5120], replicated, may hold values from -3 to 3
Outputs:
- result: bfloat16 [2, 2, 16, 128, 1280], P('fsdp', None, 'frame')
- frames_grad: bfloat16 [2, 2, 16, 128, 1280], P('fsdp', None, 'frame')
- qkv_grad: float32 [3, 1280, 1280], P(None, 'fsdp', 'frame')
- pair_grad: float32 [2, 1280, 1280], P(None, 'fsdp', 'frame')
- attn_out_grad: float32 [1280, 1280], P('fsdp', 'frame')
- ff_up_grad: float32 [1280, 5120], P('fsdp', 'frame')
- ff_down_grad: float32 [5120, 1280], P('fsdp', 'frame')
- gains_grad: float32 [3, 1280], replicated
- biases_grad: float32 [7, 1280], replicated
- up_bias_grad: float32 [5120], replicated
Inputs may be any that keep to these rules, and one draw needn't show every extreme that they name: `block_lengths`: block b of a micro-batch holds frames b * 16 to b * 16 + 15: one clip of 16 frames where its length is 16, 16 single images of length 1 where it is 1; no other lengths occur.
All inputs are finite; a program needn't handle non-finite values.
Results may differ from a plain program's by a relative error of at most 0.015.
Values may be sent and summed in bfloat16 or wider, within the bound.
No kernel may reach another device: no remote copies, remote signals or barrier semaphores. Data moves between devices by JAX's collectives and lax.ppermute only.
A program may use at most 384 MiB of HBM per device.

v0:
```python
import math

import jax
import jax.numpy as jnp
from jax import lax
from jax.sharding import PartitionSpec as P

HEADS = 8
GROUPS = 32
CLIP = 16


def pos_table(block_count, channels):
    steps_col = jnp.arange(CLIP, dtype=jnp.float32)[:, None]
    freq_rates = jnp.exp(
        jnp.arange(0, channels, 2, dtype=jnp.float32) * (-math.log(10000.0) / channels)
    )
    angles = steps_col * freq_rates[None, :]
    single = jnp.stack([jnp.sin(angles), jnp.cos(angles)], axis=-1).reshape(CLIP, channels)
    return jnp.tile(single, (block_count, 1))[:, None, :]


def norm_rows(values):
    row_mean = jnp.mean(values, axis=-1, keepdims=True)
    row_cent = values - row_mean
    row_rstd = lax.rsqrt(jnp.mean(row_cent * row_cent, axis=-1, keepdims=True) + 1e-05)
    return (row_cent * row_rstd, row_rstd)


def norm_back(grad_in, gain, row_hat, row_rstd):
    scaled = grad_in * gain
    return row_rstd * (
        scaled
        - jnp.mean(scaled, axis=-1, keepdims=True)
        - row_hat * jnp.mean(scaled * row_hat, axis=-1, keepdims=True)
    )


def outer_sum(left, right):
    return jnp.einsum("fpc,fpd->cd", left, right, preferred_element_type=jnp.float32)


def on_device(
    frames,
    cotangent,
    block_lengths,
    qkv_weight,
    pair_weight,
    attn_out_weight,
    ff_up_weight,
    ff_down_weight,
    norm_gains,
    biases,
    up_bias,
):
    local_frames = frames.shape[2]
    pixels = frames.shape[3]
    channels = frames.shape[4]
    micro_count = frames.shape[1]
    block_count = block_lengths.shape[2]
    ff_width = up_bias.shape[0]
    all_frames = block_count * CLIP
    pixel_share = pixels // lax.axis_size("frame")
    head_dim = channels // HEADS
    group_width = channels // GROUPS
    score_scale = head_dim ** (-0.5)
    head_shape = (block_count, CLIP, pixel_share, HEADS, head_dim)
    inv_root_two = 1.0 / math.sqrt(2.0)
    inv_root_tau = 1.0 / math.sqrt(2.0 * math.pi)
    frame_ids = lax.axis_index("frame") * local_frames + jnp.arange(local_frames, dtype=jnp.int32)
    block_pick = (
        frame_ids[:, None] // CLIP == jnp.arange(block_count, dtype=jnp.int32)[None, :]
    ).astype(jnp.float32)
    positions = pos_table(block_count, channels)
    diagonal = jnp.arange(CLIP)[:, None] == jnp.arange(CLIP)[None, :]
    gain_acc = jnp.zeros((3, channels), jnp.float32)
    bias_acc = jnp.zeros((7, channels), jnp.float32)
    upb_acc = jnp.zeros((ff_width,), jnp.float32)
    results = []
    input_grads = []
    kept_third, kept_branch, kept_act, kept_gthird = ([], [], [], [])
    kept_ffin, kept_gup, kept_hidden, kept_gframes = ([], [], [], [])
    kept_mixed, kept_gpixel, kept_inputs, kept_gqkv = ([], [], [], [])
    kept_copy = (
        lax.all_gather(qkv_weight, "fsdp", axis=1, tiled=True),
        lax.all_gather(pair_weight, "fsdp", axis=1, tiled=True),
        lax.all_gather(attn_out_weight, "fsdp", axis=0, tiled=True),
        lax.all_gather(ff_up_weight, "fsdp", axis=0, tiled=True),
        lax.all_gather(ff_down_weight, "fsdp", axis=0, tiled=True),
    )
    for batch_index in range(micro_count):
        qkv_full, pair_full, attn_full, up_full, down_full = kept_copy
        is_clip = block_lengths[0, batch_index] > 1
        clip_mask = jnp.sum(block_pick * is_clip.astype(jnp.float32)[None, :], axis=1)[
            :, None, None
        ]
        frame_vals = frames[0, batch_index].astype(jnp.float32)
        grouped = frame_vals.reshape(local_frames, pixels, GROUPS, group_width)
        group_mean = jnp.mean(grouped, axis=(1, 3), keepdims=True)
        centred = grouped - group_mean
        group_rstd = lax.rsqrt(jnp.mean(centred * centred, axis=(1, 3), keepdims=True) + 1e-06)
        group_hat = centred * group_rstd
        flat_hat = group_hat.reshape(local_frames, pixels, channels)
        hidden = (flat_hat * norm_gains[0] + biases[0]).astype(jnp.bfloat16)
        first_res = (
            jnp.einsum("fpc,cd->fpd", hidden, pair_full[0], preferred_element_type=jnp.float32)
            + biases[2]
        ).astype(jnp.bfloat16)
        pixel_res = lax.all_to_all(first_res, "frame", split_axis=1, concat_axis=0, tiled=True)
        res_float = pixel_res.astype(jnp.float32)
        row_hat, row_rstd = norm_rows(res_float)
        inputs = (row_hat * norm_gains[1] + biases[1] + positions).astype(jnp.bfloat16)
        projected = jnp.einsum(
            "fpc,kcd->kfpd", inputs, qkv_full, preferred_element_type=jnp.float32
        ).astype(jnp.bfloat16)
        queries = projected[0].reshape(head_shape)
        key_rows = projected[1].reshape(head_shape)
        values = projected[2].reshape(head_shape)
        scores = (
            jnp.einsum("bqphd,bkphd->bphqk", queries, key_rows, preferred_element_type=jnp.float32)
            * score_scale
        )
        allowed = jnp.logical_or(is_clip[:, None, None, None, None], diagonal)
        scores = jnp.where(allowed, scores, -1000000000.0)
        row_top = jnp.max(scores, axis=-1, keepdims=True)
        exp_scores = jnp.exp(scores - row_top)
        prob_float = exp_scores / jnp.sum(exp_scores, axis=-1, keepdims=True)
        prob_low = prob_float.astype(jnp.bfloat16)
        mixed = jnp.einsum(
            "bphqk,bkphd->bqphd", prob_low, values, preferred_element_type=jnp.float32
        )
        mixed = mixed.reshape(all_frames, pixel_share, channels).astype(jnp.bfloat16)
        attended = (
            jnp.einsum("fpc,cd->fpd", mixed, attn_full, preferred_element_type=jnp.float32)
            + biases[3]
        )
        second_res = (res_float + attended).astype(jnp.bfloat16)
        back_res = lax.all_to_all(second_res, "frame", split_axis=0, concat_axis=1, tiled=True)
        second_float = back_res.astype(jnp.float32)
        ff_hat, ff_rstd = norm_rows(second_float)
        ff_in = (ff_hat * norm_gains[2] + biases[5]).astype(jnp.bfloat16)
        up_val = (
            jnp.einsum("fpc,cd->fpd", ff_in, up_full, preferred_element_type=jnp.float32) + up_bias
        )
        act = jax.nn.gelu(up_val, approximate=False).astype(jnp.bfloat16)
        ff_out = (
            jnp.einsum("fpc,cd->fpd", act, down_full, preferred_element_type=jnp.float32)
            + biases[6]
        )
        third_res = (second_float + ff_out).astype(jnp.bfloat16)
        branch = (
            jnp.einsum("fpc,cd->fpd", third_res, pair_full[1], preferred_element_type=jnp.float32)
            + biases[4]
        )
        results.append((frame_vals + clip_mask * branch).astype(jnp.bfloat16))
        grad_out = cotangent[0, batch_index].astype(jnp.float32)
        grad_branch = (clip_mask * grad_out).astype(jnp.bfloat16)
        bias_acc = bias_acc.at[4].add(jnp.sum(grad_branch.astype(jnp.float32), axis=(0, 1)))
        grad_third = jnp.einsum(
            "fpd,cd->fpc", grad_branch, pair_full[1], preferred_element_type=jnp.float32
        ).astype(jnp.bfloat16)
        third_float = grad_third.astype(jnp.float32)
        bias_acc = bias_acc.at[6].add(jnp.sum(third_float, axis=(0, 1)))
        grad_act = jnp.einsum(
            "fpd,cd->fpc", grad_third, down_full, preferred_element_type=jnp.float32
        )
        normal_cdf = 0.5 * (1.0 + jax.scipy.special.erf(up_val * inv_root_two))
        normal_pdf = jnp.exp(-0.5 * up_val * up_val) * inv_root_tau
        grad_up = (grad_act * (normal_cdf + up_val * normal_pdf)).astype(jnp.bfloat16)
        upb_acc = upb_acc + jnp.sum(grad_up.astype(jnp.float32), axis=(0, 1))
        grad_ff_in = jnp.einsum("fpd,cd->fpc", grad_up, up_full, preferred_element_type=jnp.float32)
        gain_acc = gain_acc.at[2].add(jnp.sum(grad_ff_in * ff_hat, axis=(0, 1)))
        bias_acc = bias_acc.at[5].add(jnp.sum(grad_ff_in, axis=(0, 1)))
        grad_second = (third_float + norm_back(grad_ff_in, norm_gains[2], ff_hat, ff_rstd)).astype(
            jnp.bfloat16
        )
        grad_pixel = lax.all_to_all(grad_second, "frame", split_axis=1, concat_axis=0, tiled=True)
        bias_acc = bias_acc.at[3].add(jnp.sum(grad_pixel.astype(jnp.float32), axis=(0, 1)))
        grad_mixed = (
            jnp.einsum("fpd,cd->fpc", grad_pixel, attn_full, preferred_element_type=jnp.float32)
            .astype(jnp.bfloat16)
            .reshape(head_shape)
        )
        grad_probs = jnp.einsum(
            "bqphd,bkphd->bphqk", grad_mixed, values, preferred_element_type=jnp.float32
        )
        grad_value = jnp.einsum(
            "bphqk,bqphd->bkphd", prob_low, grad_mixed, preferred_element_type=jnp.float32
        ).astype(jnp.bfloat16)
        grad_scores = (
            prob_float * (grad_probs - jnp.sum(prob_float * grad_probs, axis=-1, keepdims=True))
        ).astype(jnp.bfloat16)
        grad_query = (
            jnp.einsum(
                "bphqk,bkphd->bqphd", grad_scores, key_rows, preferred_element_type=jnp.float32
            )
            * score_scale
        ).astype(jnp.bfloat16)
        grad_key = (
            jnp.einsum(
                "bphqk,bqphd->bkphd", grad_scores, queries, preferred_element_type=jnp.float32
            )
            * score_scale
        ).astype(jnp.bfloat16)
        grad_qkv = jnp.stack([grad_query, grad_key, grad_value]).reshape(
            3, all_frames, pixel_share, channels
        )
        grad_inputs = jnp.einsum(
            "kfpd,kcd->fpc", grad_qkv, qkv_full, preferred_element_type=jnp.float32
        )
        gain_acc = gain_acc.at[1].add(jnp.sum(grad_inputs * row_hat, axis=(0, 1)))
        bias_acc = bias_acc.at[1].add(jnp.sum(grad_inputs, axis=(0, 1)))
        grad_first = grad_pixel.astype(jnp.float32) + norm_back(
            grad_inputs, norm_gains[1], row_hat, row_rstd
        )
        grad_frames = lax.all_to_all(
            grad_first.astype(jnp.bfloat16), "frame", split_axis=0, concat_axis=1, tiled=True
        )
        bias_acc = bias_acc.at[2].add(jnp.sum(grad_frames.astype(jnp.float32), axis=(0, 1)))
        grad_hidden = jnp.einsum(
            "fpd,cd->fpc", grad_frames, pair_full[0], preferred_element_type=jnp.float32
        )
        gain_acc = gain_acc.at[0].add(jnp.sum(grad_hidden * flat_hat, axis=(0, 1)))
        bias_acc = bias_acc.at[0].add(jnp.sum(grad_hidden, axis=(0, 1)))
        group_grad = (grad_hidden * norm_gains[0]).reshape(
            local_frames, pixels, GROUPS, group_width
        )
        input_part = group_rstd * (
            group_grad
            - jnp.mean(group_grad, axis=(1, 3), keepdims=True)
            - group_hat * jnp.mean(group_grad * group_hat, axis=(1, 3), keepdims=True)
        )
        input_grads.append(
            (grad_out + input_part.reshape(local_frames, pixels, channels)).astype(jnp.bfloat16)
        )
        kept_third.append(third_res)
        kept_branch.append(grad_branch)
        kept_act.append(act)
        kept_gthird.append(grad_third)
        kept_ffin.append(ff_in)
        kept_gup.append(grad_up)
        kept_hidden.append(hidden)
        kept_gframes.append(grad_frames)
        kept_mixed.append(mixed)
        kept_gpixel.append(grad_pixel)
        kept_inputs.append(inputs)
        kept_gqkv.append(grad_qkv)
    qkv_part = jnp.einsum(
        "fpc,kfpd->kcd",
        jnp.concatenate(kept_inputs, axis=0),
        jnp.concatenate(kept_gqkv, axis=1),
        preferred_element_type=jnp.float32,
    )
    pair_part = jnp.stack(
        [
            outer_sum(jnp.concatenate(kept_hidden, axis=0), jnp.concatenate(kept_gframes, axis=0)),
            outer_sum(jnp.concatenate(kept_third, axis=0), jnp.concatenate(kept_branch, axis=0)),
        ]
    )
    attn_part = outer_sum(jnp.concatenate(kept_mixed, axis=0), jnp.concatenate(kept_gpixel, axis=0))
    up_part = outer_sum(jnp.concatenate(kept_ffin, axis=0), jnp.concatenate(kept_gup, axis=0))
    down_part = outer_sum(jnp.concatenate(kept_act, axis=0), jnp.concatenate(kept_gthird, axis=0))
    column_sums = (
        lax.psum_scatter(qkv_part, "frame", scatter_dimension=2, tiled=True),
        lax.psum_scatter(pair_part, "frame", scatter_dimension=2, tiled=True),
        lax.psum_scatter(attn_part, "frame", scatter_dimension=1, tiled=True),
        lax.psum_scatter(up_part, "frame", scatter_dimension=1, tiled=True),
        lax.psum_scatter(down_part, "frame", scatter_dimension=1, tiled=True),
    )
    qkv_own, pair_own, attn_own, up_own, down_own = (
        lax.psum_scatter(
            column_sums[0].astype(jnp.bfloat16), "fsdp", scatter_dimension=1, tiled=True
        ).astype(jnp.float32),
        lax.psum_scatter(
            column_sums[1].astype(jnp.bfloat16), "fsdp", scatter_dimension=1, tiled=True
        ).astype(jnp.float32),
        lax.psum_scatter(
            column_sums[2].astype(jnp.bfloat16), "fsdp", scatter_dimension=0, tiled=True
        ).astype(jnp.float32),
        lax.psum_scatter(
            column_sums[3].astype(jnp.bfloat16), "fsdp", scatter_dimension=0, tiled=True
        ).astype(jnp.float32),
        lax.psum_scatter(
            column_sums[4].astype(jnp.bfloat16), "fsdp", scatter_dimension=0, tiled=True
        ).astype(jnp.float32),
    )
    gain_sum, bias_sum, upb_sum = lax.psum((gain_acc, bias_acc, upb_acc), ("frame", "fsdp"))
    result = jnp.stack(results)[None]
    frames_grad = jnp.stack(input_grads)[None]
    return (
        result,
        frames_grad,
        qkv_own,
        pair_own,
        attn_own,
        up_own,
        down_own,
        gain_sum,
        bias_sum,
        upb_sum,
    )


def solution(mesh):
    placed = (
        P("fsdp", None, "frame", None, None),
        P("fsdp", None, "frame", None, None),
        P("fsdp", None, None),
        P(None, "fsdp", None),
        P(None, "fsdp", None),
        P("fsdp", None),
        P("fsdp", None),
        P("fsdp", None),
        P(),
        P(),
        P(),
    )
    return jax.shard_map(
        on_device,
        mesh=mesh,
        in_specs=placed,
        out_specs=(
            P("fsdp", None, "frame", None, None),
            P("fsdp", None, "frame", None, None),
            P(None, "fsdp", "frame"),
            P(None, "fsdp", "frame"),
            P("fsdp", "frame"),
            P("fsdp", "frame"),
            P("fsdp", "frame"),
            P(),
            P(),
            P(),
        ),
        check_vma=False,
    )
```

profile of v0, /device:TPU:8, one launch (start us, length us, event | category | flops | bytes accessed | tf_op | source)
XLA Modules:
  0.0 1846.3 jit_solution(5245182399871053672)
XLA Ops:
  16.3 77.7 %all-gather.6.cloned.1.call-done = bf16[2,1280,1280]{2,1,0:T(8,128)(2,1)} async-done(((bf16[2,640,1280]{2,1,0:T(8,128)(2,1)}), bf16[2,1280,1280]{2,1,0:T(8,128)(2,1)}) %all-gather.6.cloned.1.call-update) | async-done | bytes 6553616 | tf_op jit(solution)/shard_map/all_gather | solution.py:86
  101.1 6.1 all-to-all-start
  118.4 6.0 all-to-all-start.2
  126.4 7.4 all-to-all-done.2
  140.9 76.1 %all-gather.8.cloned.1.call-done = bf16[3,1280,1280]{2,1,0:T(8,128)(2,1)} async-done(((bf16[3,640,1280]{2,1,0:T(8,128)(2,1)}), bf16[3,1280,1280]{2,1,0:T(8,128)(2,1)}) %all-gather.8.cloned.1.call-update) | async-done | bytes 9830416 | tf_op jit(solution)/shard_map/all_gather | solution.py:85
  216.9 5.3 fusion.63
  227.1 37.8 %all-gather.10.cloned.1.call-done = bf16[1280,1280]{1,0:T(8,128)(2,1)} async-done(((bf16[640,1280]{1,0:T(8,128)(2,1)}), bf16[1280,1280]{1,0:T(8,128)(2,1)}) %all-gather.10.cloned.1.call-update) | async-done | bytes 3276816 | tf_op jit(solution)/shard_map/all_gather | solution.py:87
  268.2 6.6 all-to-all-start.1
  274.8 7.8 fusion.60
  297.5 6.4 all-to-all-start.3
  316.9 107.7 %all-gather.12.cloned.1.call-done = bf16[1280,5120]{1,0:T(8,128)(2,1)} async-done(((bf16[640,5120]{1,0:T(8,128)(2,1)}), bf16[1280,5120]{1,0:T(8,128)(2,1)}) %all-gather.12.cloned.1.call-update) | async-done | bytes 13107216 | tf_op jit(solution)/shard_map/all_gather | solution.py:88
  424.6 11.5 fusion.28
  436.2 148.2 %all-gather.14.cloned.1.call-done = bf16[5120,1280]{1,0:T(8,128)(2,1)} async-done(((bf16[2560,1280]{1,0:T(8,128)(2,1)}), bf16[5120,1280]{1,0:T(8,128)(2,1)}) %all-gather.14.cloned.1.call-update) | async-done | bytes 13107216 | tf_op jit(solution)/shard_map/all_gather | solution.py:89
  584.3 8.5 convert_reduce_fusion.1
  592.8 10.4 fusion.214
  603.3 11.7 fusion.31
  615.1 5.2 convert_reduce_fusion
  620.3 9.6 fusion.354
  634.5 4.2 reduce.160
  640.5 6.4 all-to-all-start.4
  650.5 4.2 reduce.161
  656.6 6.0 all-to-all-start.6
  678.3 4.9 convolution_bitcast_fusion.3
  717.1 11.2 convolution_bitcast_fusion.2
  730.5 10.9 convolution_bitcast_fusion.1
  743.2 10.8 convolution_bitcast_fusion
  760.1 6.8 fusion.92
  769.6 6.8 fusion.93
  778.1 4.4 convolution_bitcast_fusion.4
  786.2 4.4 multiply_reduce_fusion
  790.6 5.6 all-to-all-start.5
  799.2 6.5 all-to-all-done.5
  805.6 5.4 all-to-all-start.7
  811.9 15.2 all-to-all-done.7
  830.9 10.3 pad_maximum_fusion
  841.2 20.4 %copy.305 = f32[2,1280,1280]{1,0,2:T(2,128)} copy(f32[2,1280,1280]{2,1,0:T(8,128)} %pad_maximum_fusion) | data formatting | bytes 26214400 | tf_op jit(solution)/shard_map/stack | solution.py:254
  861.6 364.7 %all-reduce.8 = bf16[2,1280,1280]{1,0,2:T(2,128)(2,1)} all-reduce(f32[2,1280,1280]{1,0,2:T(2,128)} %copy.305), channel_id=4, replica_groups=mesh['frame'=16,'fsdp'=2] {'frame'}, use_global_device_ids=true, to_apply=%region_40.41.clone | all-reduce | flops 3276800 | bytes 19660800
  1227.5 18.1 copy.330
  1245.6 27.7 %reshape.2424 = bf16[1280,160]{1,0:T(8,128)(2,1)} reshape(bf16[1280,80,2]{2,1,0:T(8,128)(2,1)} %bitcast.539) | data formatting | bytes 819200
  1276.7 4.3 fusion.192
  1288.5 63.5 %reduce-scatter.22.cloned.1.call-done = f32[1280,320]{0,1:T(8,128)} async-done(((f32[1280,5120]{0,1:T(8,128)}), f32[1280,320]{0,1:T(8,128)}) %reduce-scatter.22.cloned.1.call-update) | async-done | bytes 1638416 | tf_op jit(solution)/shard_map/reduce_scatter | solution.py:267
  1355.5 252.7 %reduce-scatter.24.cloned.1.call-done = f32[5120,80]{0,1:T(8,128)} async-done(((f32[5120,1280]{0,1:T(8,128)}), f32[5120,80]{0,1:T(8,128)}) %reduce-scatter.24.cloned.1.call-update) | async-done | bytes 1638416 | tf_op jit(solution)/shard_map/reduce_scatter | solution.py:268
  1614.1 13.3 reduce-scatter.30.cloned.1.call-done
  1627.4 16.1 reshape.2425
  1643.5 12.5 copy.331
  1664.2 18.6 %reduce-scatter.34.cloned.1.call-done = bf16[640,320]{1,0:T(8,128)(2,1)} async-done(((bf16[1280,320]{1,0:T(8,128)(2,1)}), bf16[640,320]{1,0:T(8,128)(2,1)}) %reduce-scatter.34.cloned.1.call-update) | async-done | bytes 409616
  1685.0 18.4 reduce-scatter.26.cloned.1.call-done
  1705.3 130.0 %all-reduce.7.cloned.1.call-done = (f32[3,1280]{1,0:T(4,128)}, f32[7,1280]{1,0:T(8,128)}, f32[5120]{0:T(1024)}) async-done(((f32[3,1280]{1,0:T(4,128)}, f32[7,1280]{1,0:T(8,128)}, f32[5120]{0:T(1024)}), (f32[3,1280]{1,0:T(4,128)}, f32[7,1280]{1,0:T(8,128)}, f32[5120]{0:T(1024)})) %all-reduce.7.cloned.1.call-update) | async-done | bytes 71696 | tf_op jit(solution)/shard_map/psum | solution.py:287
  (510 shorter events, 193.5 us)
Async XLA Ops:
  7.2 86.9 %all-gather.6.cloned.1.call-start = ((), (), s32[]{:S(2)}) async-start(), calls=%async_computation.17 | async-start | bytes 9830400 | tf_op jit(solution)/shard_map/all_gather | solution.py:86
  7.9 209.0 %all-gather.8.cloned.1.call-start = ((), (), s32[]{:S(2)}) async-start(), calls=%async_computation.18 | async-start | bytes 14745600 | tf_op jit(solution)/shard_map/all_gather | solution.py:85
  8.7 256.2 %all-gather.10.cloned.1.call-start = ((), (), s32[]{:S(2)}) async-start(), calls=%async_computation.19 | async-start | bytes 4915200 | tf_op jit(solution)/shard_map/all_gather | solution.py:87
  9.4 415.2 %all-gather.12.cloned.1.call-start = ((), (), s32[]{:S(2)}) async-start(), calls=%async_computation.20 | async-start | bytes 19660800 | tf_op jit(solution)/shard_map/all_gather | solution.py:88
  10.0 574.3 %all-gather.14.cloned.1.call-start = ((), (), s32[]{:S(2)}) async-start(), calls=%async_computation.21 | async-start | bytes 19660800 | tf_op jit(solution)/shard_map/all_gather | solution.py:89
  11.5 85.1 %copy-start.59 = (f32[1280]{0:T(1024)}, f32[1280]{0:T(1024)S(1)}, u32[]{:S(2)}) copy-start(f32[1280]{0:T(1024)S(1)} %sub.306) | copy-start | bytes 15364
  11.9 95.3 %copy-start.61 = (f32[1280]{0:T(1024)}, f32[1280]{0:T(1024)S(1)}, u32[]{:S(2)}) copy-start(f32[1280]{0:T(1024)S(1)} %sub.320) | copy-start | bytes 15364
  12.5 94.7 %copy-start.64 = (f32[1280]{0:T(1024)}, f32[1280]{0:T(1024)S(1)}, u32[]{:S(2)}) copy-start(f32[1280]{0:T(1024)S(1)} %mul.771) | copy-start | bytes 15364
  13.2 94.0 %copy-start.76 = (f32[1280]{0:T(1024)}, f32[1280]{0:T(1024)S(1)}, u32[]{:S(2)}) copy-start(f32[1280]{0:T(1024)S(1)} %get-tuple-element.345) | copy-start | bytes 15364
  13.2 590.0 %copy-start.90 = (f32[1280]{0:T(1024)}, f32[1280]{0:T(1024)S(1)}, u32[]{:S(2)}) copy-start(f32[1280]{0:T(1024)S(1)} %get-tuple-element.341) | copy-start | bytes 15364
  13.3 93.9 %copy-start.66 = (f32[1280]{0:T(1024)}, f32[1280]{0:T(1024)S(1)}, u32[]{:S(2)}) copy-start(f32[1280]{0:T(1024)S(1)} %get-tuple-element.348) | copy-start | bytes 15364
  13.3 127.2 %copy-start.70 = (f32[1280]{0:T(1024)}, f32[1280]{0:T(1024)S(1)}, u32[]{:S(2)}) copy-start(f32[1280]{0:T(1024)S(1)} %get-tuple-element.349) | copy-start | bytes 15364
  13.7 82.9 %copy-start.68 = (f32[1280]{0:T(1024)}, f32[1280]{0:T(1024)S(1)}, u32[]{:S(2)}) copy-start(f32[1280]{0:T(1024)S(1)} %mul.739) | copy-start | bytes 15364
  101.1 17.3 all-to-all-start
  118.4 15.5 all-to-all-start.2
  126.4 138.5 %copy-start.9 = (f32[1,128,1280]{2,0,1:T(1,128)}, f32[1,128,1280]{2,0,1:T(1,128)S(1)}, u32[]{:S(2)}) copy-start(f32[1,128,1280]{2,0,1:T(1,128)S(1)} %bitcast_convert_fusion) | copy-start | bytes 1966084
  136.1 86.1 %copy-start.3 = (f32[1,128,1280]{2,0,1:T(1,128)}, f32[1,128,1280]{2,0,1:T(1,128)S(1)}, u32[]{:S(2)}) copy-start(f32[1,128,1280]{2,0,1:T(1,128)S(1)} %bitcast_convert_fusion.1) | copy-start | bytes 1966084
  138.2 84.0 %copy-start.80 = (f32[16,8]{1,0:T(8,128)}, f32[16,8]{1,0:T(8,128)S(1)}, u32[]{:S(2)}) copy-start(f32[16,8]{1,0:T(8,128)S(1)} %div.114) | copy-start | bytes 1540
  140.4 81.8 %copy-start.74 = (f32[16,8]{1,0:T(8,128)}, f32[16,8]{1,0:T(8,128)S(1)}, u32[]{:S(2)}) copy-start(f32[16,8]{1,0:T(8,128)S(1)} %rsqrt.60) | copy-start | bytes 1540
  140.5 81.7 %copy-start.82 = (f32[16,8]{1,0:T(8,128)}, f32[16,8]{1,0:T(8,128)S(1)}, u32[]{:S(2)}) copy-start(f32[16,8]{1,0:T(8,128)S(1)} %rsqrt.56) | copy-start | bytes 1540
  140.8 81.4 %copy-start.36 = (bf16[16,8,1280]{2,1,0:T(8,128)(2,1)}, bf16[16,8,1280]{2,1,0:T(8,128)(2,1)S(1)}, u32[]{:S(2)}) copy-start(bf16[16,8,1280]{2,1,0:T(8,128)(2,1)S(1)} %get-tuple-element.373) | copy-start | bytes 983044
  140.8 134.0 %copy-start.38 = (bf16[16,8,1280]{2,1,0:T(8,128)(2,1)}, bf16[16,8,1280]{2,1,0:T(8,128)(2,1)S(1)}, u32[]{:S(2)}) copy-start(bf16[16,8,1280]{2,1,0:T(8,128)(2,1)S(1)} %get-tuple-element.374) | copy-start | bytes 983044
  225.1 463.5 %copy-start.89 = (f32[8,8,16]{2,1,0:T(8,128)}, f32[8,8,16]{2,1,0:T(8,128)S(1)}, u32[]{:S(2)}) copy-start(f32[8,8,16]{2,1,0:T(8,128)S(1)} %get-tuple-element.390) | copy-start | bytes 12292
  268.2 29.3 %all-to-all-start.1 = ((bf16[16,8,1280]{2,1,0:T(8,128)(2,1)}), bf16[16,8,1280]{2,1,0:T(8,128)(2,1)}, u32[]{:S(2)}, u32[]{:S(2)}) async-start(bf16[16,8,1280]{2,1,0:T(8,128)(2,1)} %fusion.94), calls=%async_computation.1 | async-start | bytes 655360 | tf_op jit(solution)/shard_map/all_to_all | solution.py:138
  297.5 15.8 all-to-all-start.3
  303.9 120.8 %copy-start.106 = (f32[5120]{0:T(1024)S(1)}, f32[5120]{0:T(1024)}, u32[]{:S(2)}) copy-start(f32[5120]{0:T(1024)} %param.61) | copy-start | bytes 61444
  309.0 320.9 %copy-start.97 = (f32[128]{0:T(128)}, f32[128]{0:T(128)S(1)}, u32[]{:S(2)}) copy-start(f32[128]{0:T(128)S(1)} %div.119) | copy-start | bytes 1540
  314.5 332.5 %copy-start.95 = (f32[128]{0:T(128)}, f32[128]{0:T(128)S(1)}, u32[]{:S(2)}) copy-start(f32[128]{0:T(128)S(1)} %div.129) | copy-start | bytes 1540
  316.9 313.1 %copy-start.103 = (f32[128]{0:T(128)}, f32[128]{0:T(128)S(1)}, u32[]{:S(2)}) copy-start(f32[128]{0:T(128)S(1)} %add_rsqrt_fusion.3) | copy-start | bytes 1540
  316.9 330.0 %copy-start.101 = (f32[128]{0:T(128)}, f32[128]{0:T(128)S(1)}, u32[]{:S(2)}) copy-start(f32[128]{0:T(128)S(1)} %add_rsqrt_fusion) | copy-start | bytes 1540
  640.5 16.1 all-to-all-start.4
  656.6 15.6 all-to-all-start.6
  662.6 618.8 %reduce-scatter.20.cloned.1.call-start = ((), (), s32[]{:S(2)}) async-start(), calls=%async_computation.23 | async-start | bytes 6963200 | tf_op jit(solution)/shard_map/reduce_scatter | solution.py:266
  683.2 600.3 %reduce-scatter.18.cloned.1.call-start = ((), (), s32[]{:S(2)}) async-start(), calls=%async_computation.22 | async-start | bytes 20889600 | tf_op jit(solution)/shard_map/reduce_scatter | solution.py:264
  728.3 623.7 %reduce-scatter.22.cloned.1.call-start = ((), (), s32[]{:S(2)}) async-start(), calls=%async_computation.24 | async-start | bytes 27852800 | tf_op jit(solution)/shard_map/reduce_scatter | solution.py:267
  741.4 866.8 %reduce-scatter.24.cloned.1.call-start = ((), (), s32[]{:S(2)}) async-start(), calls=%async_computation.25 | async-start | bytes 27852800 | tf_op jit(solution)/shard_map/reduce_scatter | solution.py:268
  790.6 15.1 all-to-all-start.5
  805.6 21.5 %all-to-all-start.7 = ((bf16[16,8,1280]{2,1,0:T(8,128)(2,1)}), bf16[16,8,1280]{2,1,0:T(8,128)(2,1)S(1)}, u32[]{:S(2)}, u32[]{:S(2)}) async-start(bf16[16,8,1280]{2,1,0:T(8,128)(2,1)} %add_convert_fusion), calls=%async_computation.7 | async-start | bytes 655360 | tf_op jit(solution)/shard_map/all_to_all | solution.py:216
  811.1 816.3 %reduce-scatter.30.cloned.1.call-start = ((), (), s32[]{:S(2)}) async-start(), calls=%async_computation.28 | async-start | bytes 983040
  1273.5 383.3 %reduce-scatter.32.cloned.1.call-start = ((), (), s32[]{:S(2)}) async-start(), calls=%async_computation.29 | async-start | bytes 491520
  1283.3 377.5 %reduce-scatter.28.cloned.1.call-start = ((), (), s32[]{:S(2)}) async-start(), calls=%async_computation.27 | async-start | bytes 983040
  1287.9 394.9 %reduce-scatter.34.cloned.1.call-start = ((), (), s32[]{:S(2)}) async-start(), calls=%async_computation.30 | async-start | bytes 1474560
  1354.8 257.9 %copy-start.20 = (bf16[1,2,1,128,1280]{4,3,2,1,0:T(8,128)(2,1)S(1)}, bf16[1,2,1,128,1280]{4,3,2,1,0:T(8,128)(2,1)}, u32[]{:S(2)}) copy-start(bf16[1,2,1,128,1280]{4,3,2,1,0:T(8,128)(2,1)} %param.52) | copy-start | bytes 1966084
  1354.8 257.9 %copy-start.41 = (f32[128,1280]{1,0:T(8,128)S(1)}, f32[128,1280]{1,0:T(8,128)}, u32[]{:S(2)}) copy-start(f32[128,1280]{1,0:T(8,128)} %copy-done.40) | copy-start | bytes 1966084
  1354.8 257.9 %copy-start.42 = (f32[128,1280]{1,0:T(8,128)S(1)}, f32[128,1280]{1,0:T(8,128)}, u32[]{:S(2)}) copy-start(f32[128,1280]{1,0:T(8,128)} %get-tuple-element.401) | copy-start | bytes 1966084
  1354.9 348.5 %reduce-scatter.26.cloned.1.call-start = ((), (), s32[]{:S(2)}) async-start(), calls=%async_computation.26 | async-start | bytes 1228800 | tf_op jit(solution)/shard_map/reduce_scatter | solution.py:283
  1355.2 257.5 %copy-start.47 = (f32[7,1280]{1,0:T(8,128)}, f32[7,1280]{1,0:T(8,128)S(1)}, u32[]{:S(2)}) copy-start(f32[7,1280]{1,0:T(8,128)S(1)} %scatter-add.99) | copy-start | bytes 107524
  1610.6 224.7 %all-reduce.7.cloned.1.call-start = ((), (), s32[]{:S(2)}) async-start(), calls=%async_computation.31 | async-start | bytes 163840 | tf_op jit(solution)/shard_map/psum | solution.py:287
  (92 other events, 658.9 us)
Sparse Core Ops, SparseCore 0:
  9.6 84.4 all-gather.5
  95.6 121.2 all-gather.7
  218.5 46.3 all-gather.9
  266.3 158.2 all-gather.11
  426.0 158.2 all-gather.13
  683.3 85.6 reduce-scatter.19
  773.8 281.6 reduce-scatter.17
  1060.2 291.7 reduce-scatter.21
  1356.8 251.4 reduce-scatter.23
  1610.4 16.9 reduce-scatter.29
  1630.2 12.3 reduce-scatter.31
  1644.8 15.9 reduce-scatter.27
  1663.1 19.6 reduce-scatter.33
  1685.5 17.7 reduce-scatter.25
  1711.4 123.8 all-reduce.6
where the time goes:
time: 1860 us; the launch traced here: 1850 us
  waiting for transfers between devices  984 us (53%)
  blocking collectives  365 us (20%)
  matrix products  187 us (10%)
  local copies, waits for them, and re-layouts  178 us (10%)
  other arithmetic  65.4 us (4%)
  starting transfers between devices  49.1 us (3%)
  between operations  18.7 us (1%)
    unnamed x1, blocking collectives  365 us
    reduce_scatter x1, waiting for transfers between devices, on_device(): lax.psum_scatter(down_part, 'frame', scatter_dimension=1, tiled=True)  253 us
    all_gather x1, waiting for transfers between devices, on_device(): lax.all_gather(ff_down_weight, 'fsdp', axis=0, tiled=True)  148 us
    psum x1, waiting for transfers between devices, on_device(): lax.psum((gain_acc, bias_acc, upb_acc), ('frame', 'fsdp'))  130 us
    unnamed x262, local copies, waits for them, and re-layouts  112 us
    all_gather x1, waiting for transfers between devices, on_device(): lax.all_gather(ff_up_weight, 'fsdp', axis=0, tiled=True)  108 us
    all_gather x1, waiting for transfers between devices, on_device(): lax.all_gather(pair_weight, 'fsdp', axis=1, tiled=True)  77.7 us
    all_gather x1, waiting for transfers between devices, on_device(): lax.all_gather(qkv_weight, 'fsdp', axis=1, tiled=True)  76.1 us
  transfers between devices with their start and end apart: 23, of which 17 were waited for; matrix products, arithmetic and copies ran while one was open for 19% of the time, Pallas kernels for 0%

commit v1 on v0

v1 whole, which is shorter than its diff:
```python
import math

import jax
import jax.numpy as jnp
import numpy as np
from jax import lax
from jax.experimental import pallas as pl
from jax.experimental.pallas import tpu as pltpu
from jax.sharding import PartitionSpec as P

HEADS = 8
GROUPS = 32
CLIP = 16
CORES = 2
BF = jnp.bfloat16
F32 = jnp.float32
HIGH = lax.Precision.HIGHEST
STEP = 64
WIDE = 640


def pos_table(channels):
    steps_col = np.arange(CLIP, dtype=np.float32)[:, None]
    freq_rates = np.exp(
        np.arange(0, channels, 2, dtype=np.float32) * np.float32(-math.log(10000.0) / channels)
    )
    angles = steps_col * freq_rates[None, :]
    return np.stack([np.sin(angles), np.cos(angles)], axis=-1).reshape(CLIP, channels)


def after(value, *deps):
    return lax.optimization_barrier((value,) + deps)[0]


class Grid:
    def __init__(self, channels):
        self.nx = lax.axis_size("fsdp")
        self.nf = lax.axis_size("frame")
        chips = self.nf // CORES
        self.ny = self.nx if chips % self.nx == 0 else 1
        self.nz = chips // self.ny
        at = lax.axis_index("frame")
        self.x = lax.axis_index("fsdp")
        self.c = at % CORES
        self.y = (at // CORES) % self.ny
        z = at // (CORES * self.ny)
        self.n0 = 2 if self.nz % 2 == 0 else 1
        self.z0, self.z1 = z % self.n0, z // self.n0

        rows = channels // self.nx
        self.cores = CORES if rows % (self.ny * CORES * 16) == 0 else 1
        self.block = rows // (self.ny * self.cores)
        self.cell = self.y * self.cores + (self.c if self.cores > 1 else 0)

    def cut(self, shard, index, count, kind):
        rows, cols = shard.shape
        if kind == "tall":
            at = (self.cell * count + index) * self.block
            return lax.dynamic_slice_in_dim(shard, at, self.block, axis=0)
        width = cols // count
        part = lax.slice_in_dim(shard, index * width, (index + 1) * width, axis=1)
        return lax.dynamic_slice_in_dim(part, self.cell * self.block, self.block, axis=0)

    def size(self, axis):
        sizes = {"x": self.nx, "y": self.ny, "c": CORES, "z0": self.n0, "z1": self.nz // self.n0}
        return sizes[axis]

    def at(self, axis):
        return {"x": self.x, "y": self.y, "c": self.c, "z0": self.z0, "z1": self.z1}[axis]

    def shift(self, value, axis, off):
        size = self.size(axis)
        if axis == "x":
            return lax.ppermute(value, "fsdp", [(i, (i + off) % size) for i in range(size)])
        plane = CORES * self.ny
        step = {"c": 1, "y": CORES, "z0": plane, "z1": plane * self.n0}[axis]
        pairs = []
        for i in range(self.nf):
            place = (i // step) % size
            pairs.append((i, i + ((place + off) % size - place) * step))
        return lax.ppermute(value, "frame", pairs)

    def total(self, value):
        bit = 1
        while bit < self.nf:
            value = value + lax.ppermute(value, "frame", [(i, i ^ bit) for i in range(self.nf)])
            bit *= 2
        bit = 1
        while bit < self.nx:
            value = value + lax.ppermute(value, "fsdp", [(i, i ^ bit) for i in range(self.nx)])
            bit *= 2
        return value


class Packet:
    def __init__(self, grid, blocks, *deps):
        self.piece = jnp.stack(blocks)
        if deps:
            self.piece = after(self.piece, *deps)
        self.grid = grid

    def over_x(self):
        grid = self.grid
        self.got = {off: grid.shift(self.piece, "x", off) for off in range(1, grid.nx)}
        return list(self.got.values())

    def over_y(self, deps=(), late=()):
        grid = self.grid
        self.parts, self.mark = {}, []
        for off_x, got in self.got.items():
            got = after(got, *deps) if deps else got
            for off_y in range(grid.ny):
                over_y = grid.shift(got, "y", off_y) if off_y else got
                if off_y and late:
                    over_y = after(over_y, *late)
                for off_c in range(grid.cores):
                    over_c = grid.shift(over_y, "c", off_c) if off_c else over_y
                    self.parts[off_x, off_y, off_c] = over_c
                    if (off_y > 0) + (off_c > 0) == 1:
                        self.mark.append(over_c)
        return self.mark


class Weight:
    def __init__(self, grid, own, lead, blocks, kind):
        self.own, self.lead, self.blocks, self.kind = own, lead, blocks, kind
        self.nx, self.ny, self.cores = grid.nx, grid.ny, grid.cores
        self.rows, self.block = own.shape[1], grid.block
        self.chunks = len(blocks) if kind == "wide" else 1

    @property
    def arrays(self):
        out = [self.own]
        for packet, _ in self.blocks:
            out += list(packet.parts.values())
        return out

    def count(self):
        own = self.chunks
        return own + sum(len(packet.parts) for packet, _ in self.blocks)

    def copies(self, place, find, dst, sems, base):
        x, y, c = place[0], place[1], place[2]
        out, sem = [], base
        width = dst.shape[1] // self.chunks
        for chunk in range(self.chunks):
            cols = pl.ds(chunk * width, width)
            row = pl.multiple_of(x * self.rows, 16)
            target = dst.at[pl.ds(row, self.rows), cols]
            source = find(self.own).at[self.lead, :, cols]
            out.append([pltpu.make_async_copy(source, target, sems.at[sem])])
            sem += 1
        for at, (packet, index) in enumerate(self.blocks):
            chunk = at if self.kind == "wide" else 0
            cols = pl.ds(chunk * width, width)
            for (off_x, off_y, off_c), part in packet.parts.items():
                row = lax.rem(x + self.nx - off_x, self.nx) * self.rows
                cell = lax.rem(y + self.ny - off_y, self.ny) * self.cores
                if self.cores > 1:
                    cell = cell + lax.rem(c + CORES - off_c, CORES)
                if self.kind == "tall":
                    row = row + (cell * len(self.blocks) + at) * self.block
                else:
                    row = row + cell * self.block
                target = dst.at[pl.ds(pl.multiple_of(row, 16), self.block), cols]
                out[chunk].append(
                    pltpu.make_async_copy(find(part).at[index], target, sems.at[sem])
                )
                sem += 1
        return out


def start(copies):
    for copy in copies:
        copy.start()
    return copies


def wait(copies):
    for copy in copies:
        copy.wait()


def run(body, place, dense, weights, outs, scratch, cost):
    vmem = pl.BlockSpec(memory_space=pltpu.VMEM)
    far = {}
    for weight in weights:
        for array in weight.arrays:
            far.setdefault(id(array), array)
    order = list(far)
    count = sum(w.count() for w in weights)

    def kernel(place_ref, *refs):
        inputs, refs = refs[: len(dense)], refs[len(dense) :]
        find, refs = refs[: len(order)], refs[len(order) :]
        out_refs, scratch_refs = refs[: len(outs)], refs[len(outs) :]
        sems, base, groups = scratch_refs[-1], 0, []
        for weight, dst in zip(weights, scratch_refs):
            groups.append(
                weight.copies(place_ref, lambda a: find[order.index(id(a))], dst, sems, base)
            )
            base += weight.count()
        for group in groups:
            for copies in group:
                start(copies)
        body(inputs, groups, out_refs, scratch_refs[:-1])

    return pl.pallas_call(
        kernel,
        out_shape=[jax.ShapeDtypeStruct(shape, dtype) for shape, dtype in outs],
        in_specs=[pl.BlockSpec(memory_space=pltpu.SMEM)]
        + [vmem] * len(dense)
        + [pl.BlockSpec(memory_space=pl.ANY)] * len(order),
        out_specs=[vmem] * len(outs),
        scratch_shapes=[pltpu.VMEM(shape, dtype) for shape, dtype in scratch]
        + [pltpu.SemaphoreType.DMA((count,))],
        compiler_params=pltpu.CompilerParams(vmem_limit_bytes=60 * 2**20),
        cost_estimate=pl.CostEstimate(flops=cost * 10**9, bytes_accessed=0, transcendentals=0),
    )(place, *dense, *far.values())


def dot(left, right):
    return jnp.dot(left, right, preferred_element_type=F32)


def dot_t(left, right):
    return lax.dot_general(left, right, (((1,), (1,)), ((), ())), preferred_element_type=F32)


def dot_0(left, right):
    return lax.dot_general(left, right, (((0,), (0,)), ((), ())), preferred_element_type=F32)


def norm(values):
    cent = values - jnp.mean(values, axis=-1, keepdims=True)
    rstd = lax.rsqrt(jnp.mean(cent * cent, axis=-1, keepdims=True) + 1e-05)
    return cent * rstd, rstd


def norm_back(scaled, hat, rstd):
    return rstd * (
        scaled
        - jnp.mean(scaled, axis=-1, keepdims=True)
        - hat * jnp.mean(scaled * hat, axis=-1, keepdims=True)
    )


def fold(value):
    return jnp.sum(value.reshape(value.shape[0] // 8, 8, value.shape[1]), axis=0)


def members(channels):
    width = channels // GROUPS
    col = lax.broadcasted_iota(jnp.int32, (channels, 128), 0)
    low = lax.broadcasted_iota(jnp.int32, (channels, 128), 1) * width
    return jnp.where((col >= low) & (col < low + width), 1.0, 0.0).astype(F32)


def group_mean(partial, member, count):
    sums = jnp.broadcast_to(jnp.sum(partial, axis=0, keepdims=True), partial.shape)
    inside = jnp.dot(sums, member, precision=HIGH, preferred_element_type=F32) / count
    spread = lax.dot_general(
        inside, member, (((1,), (1,)), ((), ())), precision=HIGH, preferred_element_type=F32
    )
    return spread[:1]


def group_stats(frames, unit, pixels, member):
    channels = frames.shape[1]
    count = float(pixels * (channels // GROUPS))
    chunks = [pl.ds(unit * pixels + at, STEP) for at in range(0, pixels, STEP)]
    mean = group_mean(sum(fold(frames[rows, :].astype(F32)) for rows in chunks), member, count)
    squares = [fold(jnp.square(frames[rows, :].astype(F32) - mean)) for rows in chunks]
    rstd = lax.rsqrt(group_mean(sum(squares), member, count) + 1e-06)
    return chunks, mean, rstd, count


def enter(place, frames, gains, biases, pair0, pixels):
    tokens, channels = frames.shape

    def body(inputs, groups, outs, scratch):
        frames, gains, biases = inputs
        hidden, first = outs
        (weight,) = scratch
        member = members(channels)
        for unit in range(tokens // pixels):
            chunks, mean, rstd, _ = group_stats(frames, unit, pixels, member)
            for rows in chunks:
                hat = (frames[rows, :].astype(F32) - mean) * rstd
                hidden[rows, :] = (hat * gains[0:1, :] + biases[0:1, :]).astype(BF)
        wait(groups[0][0])
        for at in range(0, channels, WIDE):
            cols = pl.ds(at, WIDE)
            first[:, cols] = (dot(hidden[...], weight[:, cols]) + biases[2:3, cols]).astype(BF)

    square = ((tokens, channels), BF)
    return run(
        body, place, [frames, gains, biases], [pair0], [square, square],
        [((channels, channels), BF)], 7,
    )


def project(place, res, gains, biases, positions, qkv):
    tokens, channels = res.shape

    def body(inputs, groups, outs, scratch):
        res, gains, biases, positions = inputs
        rows_in = outs[0]
        for at in range(0, tokens, STEP):
            rows = pl.ds(at, STEP)
            hat, _ = norm(res[rows, :].astype(F32))
            rows_in[rows, :] = (
                hat * gains[1:2, :] + biases[1:2, :] + positions[rows, :]
            ).astype(BF)
        for k in range(3):
            wait(groups[k][0])
            for at in range(0, channels, WIDE):
                cols = pl.ds(at, WIDE)
                outs[1 + k][:, cols] = dot(rows_in[...], scratch[k][:, cols]).astype(BF)

    square = ((tokens, channels), BF)
    return run(
        body, place, [res, gains, biases, positions], qkv, [square] * 4,
        [((channels, channels), BF)] * 3, 8,
    )


def softmax(query, key, seq_col, seq_row, clip_col, scale):
    tokens = query.shape[0]
    scores = dot_t(query, key) * scale
    row = lax.broadcasted_iota(jnp.int32, (tokens, tokens), 0)
    col = lax.broadcasted_iota(jnp.int32, (tokens, tokens), 1)
    scores = jnp.where((clip_col > 0.5) | (row == col), scores, -1000000000.0)
    scores = jnp.where(seq_col == seq_row, scores, -3.0e38)
    powers = jnp.exp(scores - jnp.max(scores, axis=-1, keepdims=True))
    return powers / jnp.sum(powers, axis=-1, keepdims=True)


def attend(place, res, query, key, value, seqs, biases, attn):
    tokens, channels = res.shape
    dim = channels // HEADS

    def body(inputs, groups, outs, scratch):
        res, query, key, value, seq_col, seq_row, clip_col, biases = inputs
        mixed, second = outs
        (weight,) = scratch
        for head in range(HEADS):
            cols = slice(head * dim, head * dim + dim)
            probs = softmax(
                query[:, cols], key[:, cols], seq_col[...], seq_row[...], clip_col[...], dim**-0.5
            )
            mixed[:, cols] = dot(probs.astype(BF), value[:, cols]).astype(BF)
        wait(groups[0][0])
        for at in range(0, channels, WIDE):
            cols = pl.ds(at, WIDE)
            attended = dot(mixed[...], weight[:, cols]) + biases[3:4, cols]
            second[:, cols] = (res[:, cols].astype(F32) + attended).astype(BF)

    square = ((tokens, channels), BF)
    return run(
        body, place, [res, query, key, value, *seqs, biases], [attn], [square, square],
        [((channels, channels), BF)], 12,
    )


def ff_up(place, second, gains, biases, up_bias, up):
    tokens, channels = second.shape
    width = up_bias.shape[1]
    share = width // up.chunks

    def body(inputs, groups, outs, scratch):
        second, gains, biases, up_bias = inputs
        ff_in, act, slope = outs
        (weight,) = scratch
        for at in range(0, tokens, STEP):
            rows = pl.ds(at, STEP)
            hat, _ = norm(second[rows, :].astype(F32))
            ff_in[rows, :] = (hat * gains[2:3, :] + biases[5:6, :]).astype(BF)
        for k in range(up.chunks):
            wait(groups[0][k])

            @pl.loop(0, share // WIDE)
            def _(i):
                cols = pl.ds(pl.multiple_of(k * share + i * WIDE, 128), WIDE)
                upper = dot(ff_in[...], weight[:, cols]) + up_bias[:, cols]
                cdf = 0.5 * (1.0 + lax.erf(upper * (1.0 / math.sqrt(2.0))))
                pdf = jnp.exp(-0.5 * upper * upper) * (1.0 / math.sqrt(2.0 * math.pi))
                act[:, cols] = (upper * cdf).astype(BF)
                slope[:, cols] = cdf + upper * pdf

    return run(
        body, place, [second, gains, biases, up_bias], [up],
        [((tokens, channels), BF), ((tokens, width), BF), ((tokens, width), F32)],
        [((channels, width), BF)], 13,
    )


def ff_down(place, second, act, biases, down):
    tokens, channels = second.shape

    def body(inputs, groups, outs, scratch):
        second, act, biases = inputs
        third = outs[0]
        (weight,) = scratch
        wait(groups[0][0])
        for at in range(0, channels, WIDE):
            cols = pl.ds(at, WIDE)
            total = second[:, cols].astype(F32) + dot(act[...], weight[:, cols])
            third[:, cols] = (total + biases[6:7, cols]).astype(BF)

    return run(
        body, place, [second, act, biases], [down], [((tokens, channels), BF)],
        [((act.shape[1], channels), BF)], 11,
    )[0]


def leave(place, third, frames, mask, biases, pair1):
    tokens, channels = third.shape

    def body(inputs, groups, outs, scratch):
        third, frames, mask, biases = inputs
        (weight,) = scratch
        wait(groups[0][0])
        for at in range(0, channels, WIDE):
            cols = pl.ds(at, WIDE)
            branch = dot(third[...], weight[:, cols]) + biases[4:5, cols]
            outs[0][:, cols] = (frames[:, cols].astype(F32) + mask[...] * branch).astype(BF)

    return run(
        body, place, [third, frames, mask, biases], [pair1], [((tokens, channels), BF)],
        [((channels, channels), BF)], 5,
    )[0]


def third_back(place, cotangent, mask, pair1):
    tokens, channels = cotangent.shape

    def body(inputs, groups, outs, scratch):
        cotangent, mask = inputs
        grad_branch, grad_third, sums = outs
        weight, acc = scratch
        acc[...] = jnp.zeros_like(acc)
        for at in range(0, tokens, STEP):
            rows = pl.ds(at, STEP)
            branch = (mask[rows, :] * cotangent[rows, :].astype(F32)).astype(BF)
            grad_branch[rows, :] = branch
            acc[...] += fold(branch.astype(F32))
        sums[0:1, :] = jnp.sum(acc[...], axis=0, keepdims=True)
        wait(groups[0][0])
        for at in range(0, channels, WIDE):
            cols = pl.ds(at, WIDE)
            third = dot_t(grad_branch[...], weight[cols, :]).astype(BF)
            grad_third[:, cols] = third
            sums[1:2, cols] = jnp.sum(fold(third.astype(F32)), axis=0, keepdims=True)

    square = ((tokens, channels), BF)
    return run(
        body, place, [cotangent, mask], [pair1], [square, square, ((2, channels), F32)],
        [((channels, channels), BF), ((8, channels), F32)], 5,
    )


def ff_back(place, grad_third, second, slope, gains, down, up):
    tokens, channels = second.shape
    width = slope.shape[1]

    def body(inputs, groups, outs, scratch):
        grad_third, second, slope, gains = inputs
        grad_up, grad_second, sums, up_sum = outs
        down_w, up_w, grad_in, acc = scratch
        acc[...] = jnp.zeros_like(acc)
        wait(groups[0][0])

        @pl.loop(0, width // WIDE)
        def _(i):
            cols = pl.ds(pl.multiple_of(i * WIDE, 128), WIDE)
            grad = (dot_t(grad_third[...], down_w[cols, :]) * slope[:, cols]).astype(BF)
            grad_up[:, cols] = grad
            up_sum[:, cols] = jnp.sum(fold(grad.astype(F32)), axis=0, keepdims=True)

        for copies in groups[1]:
            wait(copies)
        for at in range(0, channels, 256):
            cols = pl.ds(at, 256)
            grad_in[:, cols] = dot_t(grad_up[...], up_w[cols, :])
        for at in range(0, tokens, STEP):
            rows = pl.ds(at, STEP)
            hat, rstd = norm(second[rows, :].astype(F32))
            grad = grad_in[rows, :]
            third = grad_third[rows, :].astype(F32)
            total = (third + norm_back(grad * gains[2:3, :], hat, rstd)).astype(BF)
            grad_second[rows, :] = total
            acc[0:8, :] += fold(grad * hat)
            acc[8:16, :] += fold(grad)
            acc[16:24, :] += fold(total.astype(F32))
        for k in range(3):
            sums[k : k + 1, :] = jnp.sum(acc[8 * k : 8 * k + 8, :], axis=0, keepdims=True)

    square = ((tokens, channels), BF)
    return run(
        body, place, [grad_third, second, slope, gains], [down, up],
        [((tokens, width), BF), square, ((3, channels), F32), ((1, width), F32)],
        [
            ((width, channels), BF), ((channels, width), BF),
            ((tokens, channels), F32), ((24, channels), F32),
        ],
        18,
    )


def attend_back(place, grad_second, res, query, key, value, seqs, gains, attn, qkv):
    tokens, channels = res.shape
    dim = channels // HEADS
    scale = dim**-0.5

    def body(inputs, groups, outs, scratch):
        grad_second, res, query, key, value, seq_col, seq_row, clip_col, gains = inputs
        grad_q, grad_k, grad_v, grad_first, sums = outs
        attn_w, qkv_w, mixed, grad_in, acc = scratch[0], scratch[1:4], *scratch[4:]
        acc[...] = jnp.zeros_like(acc)
        wait(groups[0][0])
        for at in range(0, channels, WIDE):
            cols = pl.ds(at, WIDE)
            mixed[:, cols] = dot_t(grad_second[...], attn_w[cols, :]).astype(BF)
        for head in range(HEADS):
            cols = slice(head * dim, head * dim + dim)
            q, k, v, grad = query[:, cols], key[:, cols], value[:, cols], mixed[:, cols]
            probs = softmax(q, k, seq_col[...], seq_row[...], clip_col[...], scale)
            grad_probs = dot_t(grad, v)
            grad_v[:, cols] = dot_0(probs.astype(BF), grad).astype(BF)
            inner = jnp.sum(probs * grad_probs, axis=-1, keepdims=True)
            grad_scores = (probs * (grad_probs - inner)).astype(BF)
            grad_q[:, cols] = (dot(grad_scores, k) * scale).astype(BF)
            grad_k[:, cols] = (dot_0(grad_scores, q) * scale).astype(BF)
        for k in range(3):
            wait(groups[1 + k][0])
        for at in range(0, channels, 256):
            cols = pl.ds(at, 256)
            grad_in[:, cols] = (
                dot_t(grad_q[...], qkv_w[0][cols, :])
                + dot_t(grad_k[...], qkv_w[1][cols, :])
                + dot_t(grad_v[...], qkv_w[2][cols, :])
            )
        for at in range(0, tokens, STEP):
            rows = pl.ds(at, STEP)
            hat, rstd = norm(res[rows, :].astype(F32))
            grad = grad_in[rows, :]
            total = grad_second[rows, :].astype(F32) + norm_back(grad * gains[1:2, :], hat, rstd)
            total = total.astype(BF)
            grad_first[rows, :] = total
            acc[0:8, :] += fold(grad * hat)
            acc[8:16, :] += fold(grad)
            acc[16:24, :] += fold(total.astype(F32))
        for k in range(3):
            sums[k : k + 1, :] = jnp.sum(acc[8 * k : 8 * k + 8, :], axis=0, keepdims=True)

    square = ((tokens, channels), BF)
    return run(
        body, place, [grad_second, res, query, key, value, *seqs, gains], [attn, *qkv],
        [square] * 4 + [((3, channels), F32)],
        [((channels, channels), BF)] * 4
        + [square, ((tokens, channels), F32), ((24, channels), F32)],
        17,
    )


def enter_back(place, grad_frames, frames, cotangent, gains, pair0, pixels):
    tokens, channels = frames.shape

    def body(inputs, groups, outs, scratch):
        grad_frames, frames, cotangent, gains = inputs
        out, sums = outs
        weight, grad_hidden, acc = scratch
        acc[...] = jnp.zeros_like(acc)
        member = members(channels)
        stats = [group_stats(frames, unit, pixels, member) for unit in range(tokens // pixels)]
        wait(groups[0][0])
        for at in range(0, channels, WIDE):
            cols = pl.ds(at, WIDE)
            grad_hidden[:, cols] = dot_t(grad_frames[...], weight[cols, :])
        for chunks, mean, rstd, count in stats:
            plain, cross = 0.0, 0.0
            for rows in chunks:
                hat = (frames[rows, :].astype(F32) - mean) * rstd
                grad = grad_hidden[rows, :]
                acc[0:8, :] += fold(grad * hat)
                acc[8:16, :] += fold(grad)
                plain += fold(grad * gains[0:1, :])
                cross += fold(grad * gains[0:1, :] * hat)
            plain, cross = group_mean(plain, member, count), group_mean(cross, member, count)
            for rows in chunks:
                hat = (frames[rows, :].astype(F32) - mean) * rstd
                part = rstd * (grad_hidden[rows, :] * gains[0:1, :] - plain - hat * cross)
                out[rows, :] = (cotangent[rows, :].astype(F32) + part).astype(BF)
        for k in range(2):
            sums[k : k + 1, :] = jnp.sum(acc[8 * k : 8 * k + 8, :], axis=0, keepdims=True)

    return run(
        body, place, [grad_frames, frames, cotangent, gains], [pair0],
        [((tokens, channels), BF), ((2, channels), F32)],
        [((channels, channels), BF), ((tokens, channels), F32), ((16, channels), F32)],
        11,
    )


def pick(grid, value, axis, off, dim):
    size = grid.size(axis)
    part = value.shape[dim] // size
    place = (grid.at(axis) + off) % size
    return lax.dynamic_slice_in_dim(value, place * part, part, axis=dim)


def turn(place, grads, n1, n0):
    tokens = grads[0].shape[0]

    def kernel(place_ref, *refs):
        ins, outs, scratch = refs[: len(grads)], refs[len(grads) : -1], refs[-1]
        for g, ref in enumerate(ins):
            cols = ref.shape[1]
            share = cols // (n1 * n0)
            for at in range(0, cols, WIDE):
                piece = ref[:, at : at + WIDE].astype(F32).T
                scratch[at : at + WIDE, :] = piece.astype(BF)
            for off in range(n0):
                z0 = lax.rem(place_ref[3] + off, n0)
                for z1 in range(n1):
                    rows = pl.ds(pl.multiple_of((z1 * n0 + z0) * share, 16), share)
                    base = g * n1 * share + z1 * share
                    outs[off][base : base + share, :] = scratch[rows, :]

    vmem = pl.BlockSpec(memory_space=pltpu.VMEM)
    cols = sum(grad.shape[1] for grad in grads)
    shapes = [(cols // n0, tokens)] * n0
    return pl.pallas_call(
        kernel,
        out_shape=[jax.ShapeDtypeStruct(shape, BF) for shape in shapes],
        in_specs=[pl.BlockSpec(memory_space=pltpu.SMEM)] + [vmem] * len(grads),
        out_specs=[vmem] * len(shapes),
        scratch_shapes=[pltpu.VMEM((max(grad.shape[1] for grad in grads), tokens), BF)],
        compiler_params=pltpu.CompilerParams(vmem_limit_bytes=60 * 2**20),
        cost_estimate=pl.CostEstimate(flops=cols * 10**6, bytes_accessed=0, transcendentals=0),
    )(place, *grads)


def multiply(place, rights, lefts, groups, ny):
    rows, tokens = rights[0].shape
    cols = lefts[0].shape[1]
    block = rows // (groups * ny * CORES)
    mine = rows // CORES
    count = len(rights)

    def kernel(place_ref, *refs):
        rights, lefts, out, scratch = refs[:count], refs[count : 2 * count], refs[-2], refs[-1]
        for i, ref in enumerate(rights):
            for at in range(groups * ny):
                source = pl.ds(pl.multiple_of((at * CORES + place_ref[2]) * block, 16), block)
                scratch[at * block : (at + 1) * block, i * tokens : (i + 1) * tokens] = ref[source, :]
        high = mine // max(1, mine // 320)

        @pl.loop(0, cols // WIDE)
        def _(j):
            width = pl.ds(pl.multiple_of(j * WIDE, 128), WIDE)
            for at in range(0, mine, high):
                total = 0.0
                for i, ref in enumerate(lefts):
                    cells = scratch[at : at + high, i * tokens : (i + 1) * tokens]
                    total += dot(cells, ref[:, width])
                out[at : at + high, width] = total.astype(BF)

    vmem = pl.BlockSpec(memory_space=pltpu.VMEM)
    out = pl.pallas_call(
        kernel,
        out_shape=jax.ShapeDtypeStruct((mine, cols), BF),
        in_specs=[pl.BlockSpec(memory_space=pltpu.SMEM)] + [vmem] * (2 * count),
        out_specs=vmem,
        scratch_shapes=[pltpu.VMEM((mine, count * tokens), BF)],
        compiler_params=pltpu.CompilerParams(vmem_limit_bytes=60 * 2**20),
        cost_estimate=pl.CostEstimate(
            flops=2 * mine * cols * tokens * count, bytes_accessed=0, transcendentals=0
        ),
    )(place, *rights, *lefts)
    return out.reshape(groups, ny, block, cols)


class Hop:
    def __init__(self, grid, cells, axis, dim, *deps):
        self.mine = pick(grid, cells, axis, 0, dim)
        self.got = []
        for off in range(1, grid.size(axis)):
            send = pick(grid, cells, axis, off, dim)
            self.got.append(grid.shift(after(send, *deps) if deps else send, axis, off))

    def total(self, dtype=BF):
        return sum((got.astype(F32) for got in self.got), self.mine.astype(F32)).astype(dtype)


class Share:
    def __init__(self, grid, parts, axis):
        self.own = parts[0]
        self.got = [grid.shift(part, axis, off) for off, part in enumerate(parts[1:], 1)]

    def all(self):
        return [self.own] + self.got


def over_cores(grid, arrays):
    return arrays + [grid.shift(array, "c", 1) for array in arrays]


def tie(moves, *values):
    flat = [got for move in moves for got in move.got] + list(values)
    flat = list(lax.optimization_barrier(tuple(flat)))
    for move in moves:
        move.got, flat = flat[: len(move.got)], flat[len(move.got) :]
    return flat


def on_device(
    frames,
    cotangent,
    block_lengths,
    qkv_weight,
    pair_weight,
    attn_out_weight,
    ff_up_weight,
    ff_down_weight,
    norm_gains,
    biases,
    up_bias,
):
    micro_count, local_frames, pixels, channels = frames.shape[1:]
    grid = Grid(channels)
    block_count = block_lengths.shape[2]
    all_frames = block_count * CLIP
    pixel_share = pixels // grid.nf
    group = micro_count * pixel_share
    tokens = all_frames * group
    place = jnp.stack([grid.x, grid.y, grid.c, grid.z0]).astype(jnp.int32)
    n0, n1 = grid.n0, grid.size("z1")

    def to_pixels(rows):
        parts = rows.reshape(micro_count, local_frames, grid.nf, pixel_share, channels)
        parts = parts.transpose(2, 1, 0, 3, 4)
        parts = lax.all_to_all(parts, "frame", split_axis=0, concat_axis=0, tiled=True)
        return parts.reshape(tokens, channels)

    def to_frames(rows):
        parts = rows.reshape(grid.nf, local_frames, micro_count, pixel_share, channels)
        parts = lax.all_to_all(parts, "frame", split_axis=0, concat_axis=0, tiled=True)
        return parts.transpose(2, 1, 0, 3, 4).reshape(tokens, channels)

    clip_float = (block_lengths[0] > 1).astype(F32)
    frame_ids = lax.axis_index("frame") * local_frames + jnp.arange(local_frames, dtype=jnp.int32)
    block_pick = (
        frame_ids[:, None] // CLIP == jnp.arange(block_count, dtype=jnp.int32)[None, :]
    ).astype(F32)
    frame_mask = jnp.sum(clip_float[:, None, :] * block_pick[None], axis=-1)
    frame_mask = jnp.broadcast_to(
        frame_mask[:, :, None], (micro_count, local_frames, pixels)
    ).reshape(tokens, 1)
    token_mask = jnp.broadcast_to(
        clip_float.T[:, None, :, None], (block_count, CLIP, micro_count, pixel_share)
    ).reshape(tokens, 1)
    positions = jnp.broadcast_to(
        jnp.asarray(pos_table(channels))[None, :, None, :], (block_count, CLIP, group, channels)
    ).reshape(tokens, channels)
    ids = np.arange(tokens, dtype=np.int32)
    seq_ids = ids % group + ids // (group * CLIP) * group
    seqs = [jnp.asarray(seq_ids[:, None]), jnp.asarray(seq_ids[None, :]), token_mask]
    frames_flat = frames.reshape(tokens, channels)
    cotangent_flat = cotangent.reshape(tokens, channels)

    fold_by = ff_up_weight.shape[1] // channels
    squares = [qkv_weight[k] for k in range(3)] + [attn_out_weight, pair_weight[0], pair_weight[1]]
    cuts = [grid.cut(shard, 0, 1, "square") for shard in squares]
    up_cuts = [grid.cut(ff_up_weight, k, fold_by, "wide") for k in range(fold_by)]
    down_cuts = [grid.cut(ff_down_weight, k, fold_by, "tall") for k in range(fold_by)]
    half = fold_by // 2

    packet0 = Packet(grid, [cuts[4]])
    got0 = packet0.over_x()
    packet1 = Packet(grid, cuts[:1], *got0)
    got1 = packet1.over_x()
    packet0.over_y()
    packet2 = Packet(grid, cuts[1:3], *got1)
    got2 = packet2.over_x()
    pair0 = Weight(grid, pair_weight, 0, [(packet0, 0)], "square")
    hidden, first_res = enter(place, frames_flat, norm_gains, biases, pair0, pixels)
    packet1.over_y(packet0.mark, [first_res])
    res = to_pixels(first_res)
    packet3 = Packet(grid, [cuts[3]] + up_cuts[:half], first_res, *got1)
    got3 = packet3.over_x()
    packet2.over_y(packet1.mark, [first_res])
    packet4 = Packet(grid, up_cuts[half:] + [cuts[5]], *got2, *packet1.mark)
    got4 = packet4.over_x()
    qkv = [
        Weight(grid, qkv_weight, k, [(packet2, k - 1) if k else (packet1, 0)], "square")
        for k in range(3)
    ]
    inputs, query, key, value = project(place, res, norm_gains, biases, positions, qkv)
    grad_pixels = to_pixels(after(cotangent_flat, res))

    packet3.over_y(packet2.mark, [inputs])
    attn = Weight(grid, attn_out_weight[None], 0, [(packet3, 0)], "square")
    packet5 = Packet(grid, down_cuts[:half], inputs, *got3)
    got5 = packet5.over_x()
    mixed, second_res = attend(place, res, query, key, value, seqs, biases, attn)

    packet4.over_y(packet3.mark, [second_res])
    up = Weight(
        grid, ff_up_weight[None], 0,
        [(packet3, 1 + k) for k in range(half)] + [(packet4, k) for k in range(fold_by - half)],
        "wide",
    )
    pair1 = Weight(grid, pair_weight, 1, [(packet4, fold_by - half)], "square")
    packet6 = Packet(grid, down_cuts[half:], second_res, *got4)
    packet6.over_x()
    ff_in, act, slope = ff_up(place, second_res, norm_gains, biases, up_bias[None], up)
    inputs_z = Share(grid, [after(inputs, second_res)] * n0, "z0")
    mixed_z = Share(grid, [after(mixed, second_res)] * n0, "z0")
    ff_in, act = tie([inputs_z, mixed_z], ff_in, act)
    grad_branch, grad_third, sums_third = third_back(place, grad_pixels, token_mask, pair1)

    packet5.over_y(packet4.mark, [act])
    packet6.over_y(packet4.mark, [act])
    down = Weight(
        grid, ff_down_weight[None], 0,
        [(packet5, k) for k in range(half)] + [(packet6, k) for k in range(fold_by - half)], "tall",
    )
    ny, nz = grid.ny, n1 * n0
    rows_of = lambda arrays: over_cores(grid, arrays)
    (third_turned,) = turn(place, [grad_third], n1, 1)
    down_cells = multiply(place, rows_of([third_turned]), rows_of([act]), nz, ny)

    order = [z1 * n0 + z0 for z0 in range(n0) for z1 in range(n1)]
    stages = -(-nz // 4)
    parts = [order[k * stages : (k + 1) * stages] for k in range(-(-nz // stages))]

    def down_y(k):
        return [Hop(grid, down_cells[z], "y", 0) for z in parts[k]] if k < len(parts) else []

    def down_x(hops):
        return [Hop(grid, hop.total(), "x", 2) for hop in hops]

    ffin_z = Share(grid, [ff_in] * n0, "z0")
    down_a = down_y(0)
    grad_up, grad_second, sums_ff, up_sum = ff_back(
        place, after(grad_third, down_cells), second_res, slope, norm_gains, down, up
    )
    grad_up, grad_second, down_cells = tie(down_a + [ffin_z], grad_up, grad_second, down_cells)

    down_b, down_ax = down_y(1), down_x(down_a)
    ffin4, mixed4 = rows_of(ffin_z.all()), rows_of(mixed_z.all())
    up_turn, second_turn = turn(place, [grad_up], n1, n0), turn(place, [grad_second], n1, n0)
    up_z, second_z = Share(grid, up_turn, "z0"), Share(grid, second_turn, "z0")
    grad_query, grad_key, grad_value, grad_first, sums_attn = attend_back(
        place, after(grad_second, *up_turn), res, query, key, value, seqs, norm_gains, attn, qkv
    )
    grad_query, grad_key, grad_value, grad_first, down_cells = tie(
        down_b + down_ax + [up_z, second_z], grad_query, grad_key, grad_value, grad_first, down_cells
    )

    grad_frames = to_frames(grad_first)
    down_c, down_bx = down_y(2), down_x(down_b)
    qkv_z = Share(grid, turn(place, [grad_query, grad_key, grad_value], n1, n0), "z0")
    up_cells = multiply(place, rows_of(up_z.all()), ffin4, n1, ny)
    second_cells = multiply(place, rows_of(second_z.all()), mixed4, n1, ny)
    third_res = ff_down(place, after(second_res, grad_first), act, biases, down)
    grad_frames, third_res, up_cells, second_cells, down_cells = tie(
        down_c + down_bx + [qkv_z], grad_frames, third_res, up_cells, second_cells, down_cells
    )

    down_d, down_cx = down_y(3), down_x(down_c)
    up_x = [Hop(grid, up_cells[z], "x", 2) for z in range(n1)]
    frames_grad, sums_enter = enter_back(
        place, grad_frames, frames_flat, cotangent_flat, norm_gains, pair0, pixels
    )
    qkv_right, inputs4 = rows_of(qkv_z.all()), rows_of(inputs_z.all())
    (last_turn,) = turn(place, [grad_frames], n1, 1)
    (branch_turn,) = turn(place, [grad_branch], n1, 1)
    last_right, last_left = rows_of([last_turn]), rows_of([hidden])
    branch_right, branch_left = rows_of([branch_turn]), rows_of([third_res])
    qkv_cells = multiply(place, qkv_right, inputs4, 3 * n1, ny)
    last_cells = multiply(place, last_right, last_left, nz, ny)
    branch_cells = multiply(place, branch_right, branch_left, nz, ny)
    qkv_cells, last_cells, branch_cells, third_res, frames_grad, sums_enter = tie(
        down_d + down_cx + up_x[:1],
        qkv_cells, last_cells, branch_cells, third_res, frames_grad, sums_enter,
    )

    down_dx = down_x(down_d)
    second_y = Hop(grid, second_cells, "y", 1)
    last_y = Hop(grid, last_cells, "y", 1)
    up_y = [Hop(grid, up_x[0].total(), "y", 0)]
    third_frames = to_frames(third_res)
    (qkv_cells,) = tie(down_dx + up_x[1:] + [second_y, last_y] + up_y, qkv_cells)

    qkv_x = Hop(grid, qkv_cells, "x", 3)
    up_y += [Hop(grid, hop.total(), "y", 0) for hop in up_x[1:]]
    down_parts = down_ax + down_bx + down_cx + down_dx
    down_whole = [None] * nz
    for z, hop in zip([z for part in parts for z in part], down_parts):
        down_whole[z] = hop.total()
    down_whole = jnp.stack(down_whole).reshape(n1, n0, *down_whole[0].shape[1:])
    down_z1 = Hop(grid, down_whole, "z1", 0)
    totals = [sums_third, sums_ff, sums_attn, up_sum.reshape(-1, channels), sums_enter]
    totals = grid.total(jnp.concatenate(totals, axis=0))
    (branch_cells, third_frames, totals) = tie(
        [qkv_x, down_z1] + up_y[1:], branch_cells, third_frames, totals
    )

    result = leave(place, third_frames, frames_flat, frame_mask, biases, pair1)
    branch_x = Hop(grid, branch_cells, "x", 3)
    second_x, last_x = Hop(grid, second_y.total(), "x", 3), Hop(grid, last_y.total(), "x", 3)
    qkv_y = Hop(grid, qkv_x.total(), "y", 1)
    up_whole = jnp.stack([hop.total() for hop in up_y])
    up_z1 = Hop(grid, up_whole, "z1", 0)
    down_z0 = Hop(grid, down_z1.total(), "z0", 1)
    (result,) = tie([branch_x, second_x, last_x, qkv_y, up_z1, down_z0], result)

    branch_y = Hop(grid, branch_x.total(), "y", 1)
    block = channels // grid.nf
    squares = [second_x.total().reshape(1, n1, block, -1), qkv_y.total().reshape(3, n1, block, -1)]
    squares_z1 = Hop(grid, jnp.concatenate(squares, axis=0), "z1", 1)
    last_z1 = Hop(grid, last_x.total().reshape(n1, n0, block, -1), "z1", 0)
    tie([branch_y, squares_z1, last_z1])
    branch_z1 = Hop(grid, branch_y.total().reshape(n1, n0, block, -1), "z1", 0)
    last_z0 = Hop(grid, last_z1.total(), "z0", 1)
    tie([branch_z1, last_z0])
    branch_z0 = Hop(grid, branch_z1.total(), "z0", 1)

    def own(hop, count=1):
        total = hop.total(F32)
        return total.reshape(count, -1, total.shape[-1]).transpose(0, 2, 1)

    squares_own = own(squares_z1, 4)
    attn_own, qkv_own = squares_own[0], squares_own[1:]
    up_own, down_own = own(up_z1)[0], own(down_z0)[0]
    pair_own = jnp.concatenate([own(last_z0), own(branch_z0)], axis=0)
    gain_sum = jnp.stack([totals[-2], totals[5], totals[2]])
    bias_sum = jnp.stack([totals[-1]] + [totals[k] for k in (6, 7, 4, 0, 3, 1)])
    upb_sum = totals[8:-2].reshape(-1)
    return (
        result.reshape(frames.shape),
        frames_grad.reshape(frames.shape),
        qkv_own,
        pair_own,
        attn_own,
        up_own,
        down_own,
        gain_sum,
        bias_sum,
        upb_sum,
    )


def solution(mesh):
    placed = (
        P("fsdp", None, "frame", None, None),
        P("fsdp", None, "frame", None, None),
        P("fsdp", None, None),
        P(None, "fsdp", None),
        P(None, "fsdp", None),
        P("fsdp", None),
        P("fsdp", None),
        P("fsdp", None),
        P(),
        P(),
        P(),
    )
    return jax.shard_map(
        on_device,
        mesh=mesh,
        in_specs=placed,
        out_specs=(
            P("fsdp", None, "frame", None, None),
            P("fsdp", None, "frame", None, None),
            P(None, "fsdp", "frame"),
            P(None, "fsdp", "frame"),
            P("fsdp", "frame"),
            P("fsdp", "frame"),
            P("fsdp", "frame"),
            P(),
            P(),
            P(),
        ),
        check_vma=False,
    )
```

time: 1860 us -> 599 us (0.32)
  waiting for transfers between devices: 984 us -> 211 us
  blocking collectives: 365 us -> 0 us
  matrix products: 187 us -> 0 us
  Pallas kernels: 0 us -> 182 us
  local copies, waits for them, and re-layouts: 178 us -> 62.3 us
  starting transfers between devices: 49.1 us -> 96.8 us
  other arithmetic: 65.4 us -> 34.3 us
    all_gather x5 -> x0, waiting for transfers between devices: 447 us -> none  [the longest x1 148 us: on_device(): lax.all_gather(ff_down_weight, 'fsdp', axis=0, tiled=True)]
    unnamed x1 -> x0, blocking collectives: 365 us -> none
    reduce_scatter x5 -> x0, waiting for transfers between devices: 335 us -> none  [the longest x1 253 us: on_device(): lax.psum_scatter(down_part, 'frame', scatter_dimension=1, tiled=True)]
    ppermute x0 -> x85, waiting for transfers between devices: none -> 211 us  [the longest x63 140 us: shift(): return lax.ppermute(value, 'frame', pairs)]
    dot_general x40 -> x0, matrix products: 185 us -> none  [the longest x5 34.7 us: outer_sum(): jnp.einsum('fpc,fpd->cd', left, right, preferred_element_type=jnp.float32)]
    pallas_call x0 -> x22, Pallas kernels: none -> 182 us  [the longest x10 122 us: run(): pl.pallas_call(kernel, out_shape=[jax.ShapeDtypeStruct(shape, dtype) for...]
    psum x1 -> x0, waiting for transfers between devices: 130 us -> none  [on_device(): lax.psum((gain_acc, bias_acc, upb_acc), ('frame', 'fsdp'))]
    unnamed x262 -> x110, local copies, waits for them, and re-layouts: 112 us -> 5.27 us
  transfers between devices with their start and end apart: 23 -> 89, of which waited for: 17 -> 30; matrix products, arithmetic and copies ran while one was open for 19% -> 14% of each run, Pallas kernels for 0% -> 31%
where the time goes in v1:
time: 599 us; the launch traced here: 589 us
  waiting for transfers between devices  211 us (35%)
  Pallas kernels  182 us (30%)
  starting transfers between devices  96.8 us (16%)
  local copies, waits for them, and re-layouts  62.3 us (10%)
  other arithmetic  34.3 us (6%)
    ppermute x63, waiting for transfers between devices, shift(): return lax.ppermute(value, 'frame', pairs)  140 us
    pallas_call x10, Pallas kernels, run(): pl.pallas_call(kernel, out_shape=[jax.ShapeDtypeStruct(shape, dtype) for...  122 us
    ppermute x17, waiting for transfers between devices, shift(): lax.ppermute(value, 'fsdp', [(i, (i + off) % size) for i in range(size)])  66.2 us
    ppermute x63, starting transfers between devices, shift(): return lax.ppermute(value, 'frame', pairs)  44.7 us
    pallas_call x6, Pallas kernels, multiply(): pl.pallas_call(kernel, out_shape=jax.ShapeDtypeStruct((mine, cols), BF),...  42.4 us
    ppermute x17, starting transfers between devices, shift(): lax.ppermute(value, 'fsdp', [(i, (i + off) % size) for i in range(size)])  19.8 us
    pallas_call x6, Pallas kernels, turn(): pl.pallas_call(kernel, out_shape=[jax.ShapeDtypeStruct(shape, BF) for sha...  17.5 us
    dynamic_slice x26, local copies, waits for them, and re-layouts, pick(): return lax.dynamic_slice_in_dim(value, place * part, part, axis=dim)  17.4 us
  transfers between devices with their start and end apart: 89, of which 30 were waited for; matrix products, arithmetic and copies ran while one was open for 14% of the time, Pallas kernels for 31%

profile of v1, /device:TPU:8, one launch (start us, length us, event | category | flops | bytes accessed | tf_op | source)
XLA Modules:
  0.0 589.0 jit_solution(7662171399834072997)
XLA Ops:
  0.7 4.0 fusion.21
  7.3 2.7 fusion.19
  12.4 4.8 collective-permute-done.refs_4_.refs_5_
  21.1 6.7 %collective-permute-done.2.refs_6_.refs_7_ = bf16[1,160,1280]{2,1,0:T(8,128)(2,1)} collective-permute-done((bf16[1,160,1280]{2,1,0:T(8,128)(2,1)}, bf16[1,160,1280]{2,1,0:T(8,128)(2,1)}, u32[]{:S(2)}, u32[]{:S(2)}) %collective-permute-start.2) | collective-permute-done | bytes 409632 | tf_op jit(solution)/shard_map/ppermute | solution.py:81
  32.7 7.1 %shard_map.213 = (bf16[256,1280]{1,0:T(8,128)(2,1)}, bf16[256,1280]{1,0:T(8,128)(2,1)}) custom-call(s32[4]{0:T(128)} %pad_add_fusion.place_ref, bf16[256,1280]{1,0:T(8,128)(2,1)} %bitcast.179, f32[3,1280]{1,0:T(4,128)} %refs_3_.6, f32[7,1280]{1,0:T(8,128)} %refs_3_.7, bf16[2,640,1280]{2,1,0:T(8,128)(2,1)} %refs_4_.6, ...), custom_call_target="tpu_custom_call" | custom-call | flops 7000000000 | tf_op jit(solution)/shard_map/pallas_call | solution.py:208
  40.5 2.6 collective-permute-done.7.refs_7_.refs_17_
  43.1 8.0 %collective-permute-done.5.refs_9_.refs_19_ = bf16[2,160,1280]{2,1,0:T(8,128)(2,1)S(1)} collective-permute-done((bf16[2,160,1280]{2,1,0:T(8,128)(2,1)S(1)}, bf16[2,160,1280]{2,1,0:T(8,128)(2,1)S(1)}, u32[]{:S(2)}, u32[]{:S(2)}) %collective-permute-start.5) | collective-permute-done | bytes 819232 | tf_op jit(solution)/shard_map/ppermute | solution.py:74
  53.6 6.7 %all-to-all-start = ((bf16[16,1,2,8,1280]{4,3,2,1,0:T(8,128)(2,1)}), bf16[16,1,2,8,1280]{4,3,2,1,0:T(8,128)(2,1)S(1)}, u32[]{:S(2)}, u32[]{:S(2)}) async-start(bf16[16,1,2,8,1280]{4,3,2,1,0:T(8,128)(2,1)} %bitcast.137), calls=%async_computation | async-start | bytes 1310720 | tf_op jit(solution)/shard_map/all_to_all | solution.py:744
  60.4 14.4 %collective-permute-done.11.refs_11_.refs_21_ = bf16[2,160,1280]{2,1,0:T(8,128)(2,1)} collective-permute-done((bf16[2,160,1280]{2,1,0:T(8,128)(2,1)S(1)}, bf16[2,160,1280]{2,1,0:T(8,128)(2,1)}, u32[]{:S(2)}, u32[]{:S(2)}) %collective-permute-start.11) | collective-permute-done | bytes 819232 | tf_op jit(solution)/shard_map/ppermute | solution.py:81
  82.5 8.0 %shard_map.214 = (bf16[256,1280]{1,0:T(8,128)(2,1)}, bf16[256,1280]{1,0:T(8,128)(2,1)}, bf16[256,1280]{1,0:T(8,128)(2,1)}, bf16[256,1280]{1,0:T(8,128)(2,1)}) custom-call(s32[4]{0:T(128)} %pad_add_fusion.place_ref, bf16[256,1280]{1,0:T(8,128)(2,1)} %bitcast.167, f32[3,1280]{1,0:T(4,128)} %refs_3_.6, f32[7,1280]{1,0:T(8,128)} %refs_3_.7, ...), custom_call_target="tpu_custom_call" | custom-call | flops 8000000000 | tf_op jit(solution)/shard_map/pallas_call | solution.py:208
  90.5 15.4 %collective-permute-done.13.refs_11_.refs_7_.refs_16_.refs_12_ = bf16[3,160,1280]{2,1,0:T(8,128)(2,1)} collective-permute-done((bf16[3,160,1280]{2,1,0:T(8,128)(2,1)}, bf16[3,160,1280]{2,1,0:T(8,128)(2,1)}, u32[]{:S(2)}, u32[]{:S(2)}) %collective-permute-start.13) | collective-permute-done | bytes 1228832 | tf_op jit(solution)/shard_map/ppermute | solution.py:81
  109.6 12.6 %shard_map.215 = (bf16[256,1280]{1,0:T(8,128)(2,1)}, bf16[256,1280]{1,0:T(8,128)(2,1)}) custom-call(s32[4]{0:T(128)} %pad_add_fusion.place_ref, bf16[256,1280]{1,0:T(8,128)(2,1)} %bitcast.168, bf16[256,1280]{1,0:T(8,128)(2,1)} %get-tuple-element.138.refs_1_.refs_2_, bf16[256,1280]{1,0:T(8,128)(2,1)} %get-tuple-element.139.refs_2_.refs_3_, ...), custom_call_target="tpu_custom_call" | custom-call | flops 12000000000 | tf_op jit(solution)/shard_map/pallas_call | solution.py:208
  122.2 14.3 %collective-permute-done.17.refs_5_.refs_11_.refs_20_.refs_7_ = bf16[3,160,1280]{2,1,0:T(8,128)(2,1)S(1)} collective-permute-done((bf16[3,160,1280]{2,1,0:T(8,128)(2,1)}, bf16[3,160,1280]{2,1,0:T(8,128)(2,1)S(1)}, u32[]{:S(2)}, u32[]{:S(2)}) %collective-permute-start.17) | collective-permute-done | bytes 1228832 | tf_op jit(solution)/shard_map/ppermute | solution.py:81
  139.6 25.6 %shard_map.218 = (bf16[256,1280]{1,0:T(8,128)(2,1)}, bf16[256,5120]{1,0:T(8,128)(2,1)}, f32[256,5120]{1,0:T(8,128)}) custom-call(s32[4]{0:T(128)} %pad_add_fusion.place_ref, bf16[256,1280]{1,0:T(8,128)(2,1)} %get-tuple-element.179.refs_0_.refs_1_, f32[3,1280]{1,0:T(4,128)} %refs_3_.6, f32[7,1280]{1,0:T(8,128)} %refs_3_.7, f32[1,5120]{1,0:T(1,128)} %bitcast.182, ...), custom_call_target="tpu_custom_call" | custom-call | flops 12999999488 | tf_op jit(solution)/shard_map/pallas_call | solution.py:208
  165.2 2.6 collective-permute-done.22.refs_5_
  171.1 6.1 %all-to-all-start.1 = ((bf16[16,1,2,8,1280]{4,3,2,1,0:T(8,128)(2,1)}), bf16[16,1,2,8,1280]{4,3,2,1,0:T(8,128)(2,1)}, u32[]{:S(2)}, u32[]{:S(2)}) async-start(bf16[16,1,2,8,1280]{4,3,2,1,0:T(8,128)(2,1)} %bitcast.136), calls=%async_computation.1 | async-start | bytes 1310720 | tf_op jit(solution)/shard_map/all_to_all | solution.py:744
  180.6 19.0 %collective-permute-done.26.refs_5_.refs_4_ = bf16[2,160,1280]{2,1,0:T(8,128)(2,1)} collective-permute-done((bf16[2,160,1280]{2,1,0:T(8,128)(2,1)S(1)}, bf16[2,160,1280]{2,1,0:T(8,128)(2,1)}, u32[]{:S(2)}, u32[]{:S(2)}) %collective-permute-start.26) | collective-permute-done | bytes 819232 | tf_op jit(solution)/shard_map/ppermute | solution.py:74
  201.1 15.3 %collective-permute-done.30.refs_9_.refs_8_ = bf16[2,160,1280]{2,1,0:T(8,128)(2,1)} collective-permute-done((bf16[2,160,1280]{2,1,0:T(8,128)(2,1)S(1)}, bf16[2,160,1280]{2,1,0:T(8,128)(2,1)}, u32[]{:S(2)}, u32[]{:S(2)}) %collective-permute-start.30) | collective-permute-done | bytes 819232 | tf_op jit(solution)/shard_map/ppermute | solution.py:74
  217.9 5.1 shard_map.216
  228.8 7.4 %collective-permute-done.32.refs_11_.refs_10_ = bf16[2,160,1280]{2,1,0:T(8,128)(2,1)} collective-permute-done((bf16[2,160,1280]{2,1,0:T(8,128)(2,1)}, bf16[2,160,1280]{2,1,0:T(8,128)(2,1)}, u32[]{:S(2)}, u32[]{:S(2)}) %collective-permute-start.32) | collective-permute-done | bytes 819232 | tf_op jit(solution)/shard_map/ppermute | solution.py:81
  238.2 11.2 %shard_map.219 = bf16[640,5120]{1,0:T(8,128)(2,1)} custom-call(s32[4]{0:T(128)} %pad_add_fusion.place_ref, bf16[1280,256]{1,0:T(8,128)(2,1)} %shard_map.217.refs_0_, bf16[1280,256]{1,0:T(8,128)(2,1)} %copy-done.33, bf16[256,5120]{1,0:T(8,128)(2,1)} %get-tuple-element.148.refs_2_.refs_1_, bf16[256,5120]{1,0:T(8,128)(2,1)} %copy-done.21), custom_call_target="tpu_custom_call" | custom-call | flops 3355443200 | tf_op jit(solution)/shard_map/pallas_call | solution.py:671
  253.2 18.9 %shard_map.220 = (bf16[256,5120]{1,0:T(8,128)(2,1)}, bf16[256,1280]{1,0:T(8,128)(2,1)}, f32[3,1280]{1,0:T(4,128)}, f32[1,5120]{1,0:T(1,128)}) custom-call(s32[4]{0:T(128)} %pad_add_fusion.place_ref, bf16[256,1280]{1,0:T(8,128)(2,1)} %get-tuple-element.150.refs_0_, bf16[256,1280]{1,0:T(8,128)(2,1)} %get-tuple-element.179.refs_0_.refs_1_, ...), custom_call_target="tpu_custom_call" | custom-call | flops 17999998976 | tf_op jit(solution)/shard_map/pallas_call | solution.py:208
  274.2 4.5 shard_map.221
  287.8 16.9 %shard_map.223 = (bf16[256,1280]{1,0:T(8,128)(2,1)}, bf16[256,1280]{1,0:T(8,128)(2,1)}, bf16[256,1280]{1,0:T(8,128)(2,1)}, bf16[256,1280]{1,0:T(8,128)(2,1)}, f32[3,1280]{1,0:T(4,128)}) custom-call(s32[4]{0:T(128)} %pad_add_fusion.place_ref, bf16[256,1280]{1,0:T(8,128)(2,1)} %get-tuple-element.167.refs_0_, bf16[256,1280]{1,0:T(8,128)(2,1)} %bitcast.169, ...), custom_call_target="tpu_custom_call" | custom-call | flops 16999999488 | tf_op jit(solution)/shard_map/pallas_call | solution.py:208
  304.7 11.6 %collective-permute-done.37.refs_1_ = bf16[640,256]{1,0:T(8,128)(2,1)} collective-permute-done((bf16[640,256]{1,0:T(8,128)(2,1)}, bf16[640,256]{1,0:T(8,128)(2,1)}, u32[]{:S(2)}, u32[]{:S(2)}) %collective-permute-start.37) | collective-permute-done | bytes 327712 | tf_op jit(solution)/shard_map/ppermute | solution.py:81
  318.5 5.6 all-to-all-start.2
  324.0 11.8 %shard_map.225.refs_2_ = bf16[256,1280]{1,0:T(8,128)(2,1)} custom-call(s32[4]{0:T(128)} %pad_add_fusion.place_ref, bf16[256,1280]{1,0:T(8,128)(2,1)} %get-tuple-element.179.refs_0_.refs_1_, bf16[256,5120]{1,0:T(8,128)(2,1)} %get-tuple-element.148.refs_2_.refs_1_, f32[7,1280]{1,0:T(8,128)} %refs_3_.7, bf16[1,2560,1280]{2,1,0:T(8,128)(2,1)} %bitcast.175, ...), custom_call_target="tpu_custom_call" | custom-call | flops 11000000512 | tf_op jit(solution)/shard_map/pallas_call | solution.py:208
  338.6 4.0 shard_map.224
  349.5 4.4 shard_map.227
  356.5 9.9 %shard_map.226 = bf16[1280,1280]{1,0:T(8,128)(2,1)} custom-call(s32[4]{0:T(128)} %pad_add_fusion.place_ref, bf16[2560,256]{1,0:T(8,128)(2,1)} %get-tuple-element.166.refs_0_, bf16[2560,256]{1,0:T(8,128)(2,1)} %collective-permute-done.36.refs_1_, bf16[2560,256]{1,0:T(8,128)(2,1)} %collective-permute-done.41.refs_2_, ...), custom_call_target="tpu_custom_call" | custom-call | flops 3355443200 | tf_op jit(solution)/shard_map/pallas_call | solution.py:671
  368.8 3.4 fusion.20
  377.2 11.2 %shard_map.233 = (bf16[256,1280]{1,0:T(8,128)(2,1)}, f32[2,1280]{1,0:T(2,128)}) custom-call(s32[4]{0:T(128)} %pad_add_fusion.place_ref, bf16[256,1280]{1,0:T(8,128)(2,1)} %bitcast.171, bf16[256,1280]{1,0:T(8,128)(2,1)} %bitcast.180, bf16[256,1280]{1,0:T(8,128)(2,1)} %bitcast.165, f32[3,1280]{1,0:T(4,128)} %refs_3_.6, bf16[2,640,1280]{2,1,0:T(8,128)(2,1)} %refs_4_.6, ...), custom_call_target="tpu_custom_call" | custom-call | flops 11000000512 | tf_op jit(solution)/shard_map/pallas_call | solution.py:208
  400.8 4.4 shard_map.232
  405.2 4.3 shard_map.230
  411.6 8.2 %shard_map.228 = bf16[960,1280]{1,0:T(8,128)(2,1)} custom-call(s32[4]{0:T(128)} %pad_add_fusion.place_ref, bf16[1920,256]{1,0:T(8,128)(2,1)} %get-tuple-element.188.refs_0_, bf16[1920,256]{1,0:T(8,128)(2,1)} %collective-permute-done.40.refs_1_, bf16[1920,256]{1,0:T(8,128)(2,1)} %collective-permute-done.52.refs_2_, ...), custom_call_target="tpu_custom_call" | custom-call | flops 2516582400 | tf_op jit(solution)/shard_map/pallas_call | solution.py:671
  419.8 5.8 collective-permute-done.50
  441.3 2.8 collective-permute-done.71
  446.3 7.5 %all-to-all-start.3 = ((bf16[16,1,2,8,1280]{4,3,2,1,0:T(8,128)(2,1)}), bf16[16,1,2,8,1280]{4,3,2,1,0:T(8,128)(2,1)}, u32[]{:S(2)}, u32[]{:S(2)}) async-start(bf16[16,1,2,8,1280]{4,3,2,1,0:T(8,128)(2,1)} %bitcast.54), calls=%async_computation.3 | async-start | bytes 1310720 | tf_op jit(solution)/shard_map/all_to_all | solution.py:749
  455.8 9.8 %collective-permute-done.60 = bf16[1,80,2560]{2,1,0:T(8,128)(2,1)S(1)} collective-permute-done((bf16[1,80,2560]{2,1,0:T(8,128)(2,1)}, bf16[1,80,2560]{2,1,0:T(8,128)(2,1)S(1)}, u32[]{:S(2)}, u32[]{:S(2)}) %collective-permute-start.60) | collective-permute-done | bytes 409632 | tf_op jit(solution)/shard_map/ppermute | solution.py:74
  484.6 23.0 %collective-permute-done.66 = bf16[1,2,80,2560]{3,2,1,0:T(8,128)(2,1)} collective-permute-done((bf16[1,2,80,2560]{3,2,1,0:T(8,128)(2,1)}, bf16[1,2,80,2560]{3,2,1,0:T(8,128)(2,1)}, u32[]{:S(2)}, u32[]{:S(2)}) %collective-permute-start.66) | collective-permute-done | bytes 819232 | tf_op jit(solution)/shard_map/ppermute | solution.py:81
  522.8 5.3 shard_map.234
  528.1 11.8 %collective-permute-done.77 = bf16[1,1,320,640]{3,2,1,0:T(8,128)(2,1)} collective-permute-done((bf16[1,1,320,640]{3,2,1,0:T(8,128)(2,1)S(1)}, bf16[1,1,320,640]{3,2,1,0:T(8,128)(2,1)}, u32[]{:S(2)}, u32[]{:S(2)}) %collective-permute-start.77) | collective-permute-done | bytes 409632 | tf_op jit(solution)/shard_map/ppermute | solution.py:81
  541.2 3.6 collective-permute-start.81
  553.9 7.4 %collective-permute-done.81 = bf16[1,2,80,640]{3,2,1,0:T(8,128)(2,1)S(1)} collective-permute-done((bf16[1,2,80,640]{3,2,1,0:T(8,128)(2,1)S(1)}, bf16[1,2,80,640]{3,2,1,0:T(8,128)(2,1)S(1)}, u32[]{:S(2)}, u32[]{:S(2)}) %collective-permute-start.81) | collective-permute-done | bytes 204832 | tf_op jit(solution)/shard_map/ppermute | solution.py:81
  561.3 8.7 %collective-permute-done.80 = bf16[4,1,80,640]{3,2,1,0:T(8,128)(2,1)S(1)} collective-permute-done((bf16[4,1,80,640]{3,2,1,0:T(8,128)(2,1)S(1)}, bf16[4,1,80,640]{3,2,1,0:T(8,128)(2,1)S(1)}, u32[]{:S(2)}, u32[]{:S(2)}) %collective-permute-start.80) | collective-permute-done | bytes 409632 | tf_op jit(solution)/shard_map/ppermute | solution.py:81
  576.6 6.1 %collective-permute-done.82 = bf16[1,2,80,640]{3,2,1,0:T(8,128)(2,1)S(1)} collective-permute-done((bf16[1,2,80,640]{3,2,1,0:T(8,128)(2,1)S(1)}, bf16[1,2,80,640]{3,2,1,0:T(8,128)(2,1)S(1)}, u32[]{:S(2)}, u32[]{:S(2)}) %collective-permute-start.82) | collective-permute-done | bytes 204832 | tf_op jit(solution)/shard_map/ppermute | solution.py:81
  582.8 2.5 collective-permute-start.84
  585.4 2.6 collective-permute-done.84
  (371 shorter events, 171.4 us)
Async XLA Ops:
  39.9 36.7 %collective-permute-start.9 = (bf16[3,160,1280]{2,1,0:T(8,128)(2,1)S(1)}, bf16[3,160,1280]{2,1,0:T(8,128)(2,1)}, u32[]{:S(2)}, u32[]{:S(2)}) collective-permute-start(bf16[3,160,1280]{2,1,0:T(8,128)(2,1)S(1)} %pad_maximum_fusion.2), channel_id=1, source_target_pairs={{0,1},{1,0},{2,3},{3,2},{4,5},{5,4},{6,7},{7,6},{8,9},{9,8},{10,11... | collective-permute-start | bytes 3686408 | tf_op jit(solution)/shard_map/ppermute | solution.py:74
  51.1 23.7 %collective-permute-start.11 = (bf16[2,160,1280]{2,1,0:T(8,128)(2,1)S(1)}, bf16[2,160,1280]{2,1,0:T(8,128)(2,1)}, u32[]{:S(2)}, u32[]{:S(2)}) collective-permute-start(bf16[2,160,1280]{2,1,0:T(8,128)(2,1)S(1)} %collective-permute-done.5.refs_9_.refs_19_), channel_id=1, source_target_pairs={{0,4},{2,6},{4,0},{6,2},{8,12},{10,14},{12,8},{14,10},{16,20},{18,... | collective-permute-start | bytes 2457608 | tf_op jit(solution)/shard_map/ppermute | solution.py:81
  51.7 24.9 %collective-permute-start.10 = (bf16[2,160,1280]{2,1,0:T(8,128)(2,1)S(1)}, bf16[2,160,1280]{2,1,0:T(8,128)(2,1)}, u32[]{:S(2)}, u32[]{:S(2)}) collective-permute-start(bf16[2,160,1280]{2,1,0:T(8,128)(2,1)S(1)} %collective-permute-done.5.refs_9_.refs_19_), channel_id=1, source_target_pairs={{0,2},{2,0},{4,6},{6,4},{8,10},{10,8},{12,14},{14,12},{16,18},{18,... | collective-permute-start | bytes 2457608 | tf_op jit(solution)/shard_map/ppermute | solution.py:81
  53.6 27.5 %all-to-all-start = ((bf16[16,1,2,8,1280]{4,3,2,1,0:T(8,128)(2,1)}), bf16[16,1,2,8,1280]{4,3,2,1,0:T(8,128)(2,1)S(1)}, u32[]{:S(2)}, u32[]{:S(2)}) async-start(bf16[16,1,2,8,1280]{4,3,2,1,0:T(8,128)(2,1)} %bitcast.137), calls=%async_computation | async-start | bytes 1310720 | tf_op jit(solution)/shard_map/all_to_all | solution.py:744
  76.6 29.3 %collective-permute-start.13 = (bf16[3,160,1280]{2,1,0:T(8,128)(2,1)}, bf16[3,160,1280]{2,1,0:T(8,128)(2,1)}, u32[]{:S(2)}, u32[]{:S(2)}) collective-permute-start(bf16[3,160,1280]{2,1,0:T(8,128)(2,1)} %collective-permute-done.9.refs_9_.refs_5_.refs_14_.refs_10_), channel_id=1, source_target_pairs={{0,4},{2,6},{4,0},{6,2},{8,12},{10,14},{12,8},{14,10},{16,20},{18,... | collective-permute-start | bytes 3686408 | tf_op jit(solution)/shard_map/ppermute | solution.py:81
  79.5 28.9 %collective-permute-start.8 = (bf16[3,160,1280]{2,1,0:T(8,128)(2,1)S(1)}, bf16[3,160,1280]{2,1,0:T(8,128)(2,1)}, u32[]{:S(2)}, u32[]{:S(2)}) collective-permute-start(bf16[3,160,1280]{2,1,0:T(8,128)(2,1)S(1)} %pad_maximum_fusion.1), channel_id=1, source_target_pairs={{0,1},{1,0},{2,3},{3,2},{4,5},{5,4},{6,7},{7,6},{8,9},{9,8},{10,11... | collective-permute-start | bytes 3686408 | tf_op jit(solution)/shard_map/ppermute | solution.py:74
  81.1 27.4 %collective-permute-start.12 = (bf16[3,160,1280]{2,1,0:T(8,128)(2,1)}, bf16[3,160,1280]{2,1,0:T(8,128)(2,1)}, u32[]{:S(2)}, u32[]{:S(2)}) collective-permute-start(bf16[3,160,1280]{2,1,0:T(8,128)(2,1)} %collective-permute-done.9.refs_9_.refs_5_.refs_14_.refs_10_), channel_id=1, source_target_pairs={{0,2},{2,0},{4,6},{6,4},{8,10},{10,8},{12,14},{14,12},{16,18},{18,... | collective-permute-start | bytes 3686408 | tf_op jit(solution)/shard_map/ppermute | solution.py:81
  108.4 28.1 %collective-permute-start.17 = (bf16[3,160,1280]{2,1,0:T(8,128)(2,1)}, bf16[3,160,1280]{2,1,0:T(8,128)(2,1)S(1)}, u32[]{:S(2)}, u32[]{:S(2)}) collective-permute-start(bf16[3,160,1280]{2,1,0:T(8,128)(2,1)} %collective-permute-done.8.refs_3_.refs_9_.refs_18_.refs_5_), channel_id=1, source_target_pairs={{0,4},{2,6},{4,0},{6,2},{8,12},{10,14},{12,8},{14,10},{16,20},{18,... | collective-permute-start | bytes 3686408 | tf_op jit(solution)/shard_map/ppermute | solution.py:81
  109.6 29.0 %collective-permute-start.16 = (bf16[3,160,1280]{2,1,0:T(8,128)(2,1)}, bf16[3,160,1280]{2,1,0:T(8,128)(2,1)S(1)}, u32[]{:S(2)}, u32[]{:S(2)}) collective-permute-start(bf16[3,160,1280]{2,1,0:T(8,128)(2,1)} %collective-permute-done.8.refs_3_.refs_9_.refs_18_.refs_5_), channel_id=1, source_target_pairs={{0,2},{2,0},{4,6},{6,4},{8,10},{10,8},{12,14},{14,12},{16,18},{18,... | collective-permute-start | bytes 3686408 | tf_op jit(solution)/shard_map/ppermute | solution.py:81
  136.5 28.7 %collective-permute-start.21 = (bf16[256,1280]{1,0:T(8,128)(2,1)S(1)}, bf16[256,1280]{1,0:T(8,128)(2,1)}, u32[]{:S(2)}, u32[]{:S(2)}) collective-permute-start(bf16[256,1280]{1,0:T(8,128)(2,1)S(1)} %copy-done.49), channel_id=1, source_target_pairs={{0,8},{2,10},{4,12},{6,14},{8,0},{10,2},{12,4},{14,6},{16,24},{18,... | collective-permute-start | bytes 1966088 | tf_op jit(solution)/shard_map/ppermute | solution.py:81
  137.1 30.7 %collective-permute-start.22 = (bf16[256,1280]{1,0:T(8,128)(2,1)}, bf16[256,1280]{1,0:T(8,128)(2,1)}, u32[]{:S(2)}, u32[]{:S(2)}) collective-permute-start(bf16[256,1280]{1,0:T(8,128)(2,1)} %get-tuple-element.145.refs_4_), channel_id=1, source_target_pairs={{0,8},{2,10},{4,12},{6,14},{8,0},{10,2},{12,4},{14,6},{16,24},{18,... | collective-permute-start | bytes 1966088 | tf_op jit(solution)/shard_map/ppermute | solution.py:81
  167.8 68.9 %collective-permute-start.23 = (bf16[256,5120]{1,0:T(8,128)(2,1)}, bf16[256,5120]{1,0:T(8,128)(2,1)S(1)}, u32[]{:S(2)}, u32[]{:S(2)}) collective-permute-start(bf16[256,5120]{1,0:T(8,128)(2,1)} %get-tuple-element.148.refs_2_.refs_1_), channel_id=1, source_target_pairs={{0,2},{2,0},{4,6},{6,4},{8,10},{10,8},{12,14},{14,12},{16,18},{18,... | collective-permute-start | bytes 7864328 | tf_op jit(solution)/shard_map/ppermute | solution.py:81
  171.1 46.8 %all-to-all-start.1 = ((bf16[16,1,2,8,1280]{4,3,2,1,0:T(8,128)(2,1)}), bf16[16,1,2,8,1280]{4,3,2,1,0:T(8,128)(2,1)}, u32[]{:S(2)}, u32[]{:S(2)}) async-start(bf16[16,1,2,8,1280]{4,3,2,1,0:T(8,128)(2,1)} %bitcast.136), calls=%async_computation.1 | async-start | bytes 1310720 | tf_op jit(solution)/shard_map/all_to_all | solution.py:744
  180.0 36.4 %collective-permute-start.30 = (bf16[2,160,1280]{2,1,0:T(8,128)(2,1)S(1)}, bf16[2,160,1280]{2,1,0:T(8,128)(2,1)}, u32[]{:S(2)}, u32[]{:S(2)}) collective-permute-start(bf16[2,160,1280]{2,1,0:T(8,128)(2,1)S(1)} %pad_maximum_fusion.5), channel_id=1, source_target_pairs={{0,1},{1,0},{2,3},{3,2},{4,5},{5,4},{6,7},{7,6},{8,9},{9,8},{10,11... | collective-permute-start | bytes 2457608 | tf_op jit(solution)/shard_map/ppermute | solution.py:74
  199.7 26.9 %collective-permute-start.28 = (bf16[2,160,1280]{2,1,0:T(8,128)(2,1)}, bf16[2,160,1280]{2,1,0:T(8,128)(2,1)}, u32[]{:S(2)}, u32[]{:S(2)}) collective-permute-start(bf16[2,160,1280]{2,1,0:T(8,128)(2,1)} %collective-permute-done.26.refs_5_.refs_4_), channel_id=1, source_target_pairs={{0,4},{2,6},{4,0},{6,2},{8,12},{10,14},{12,8},{14,10},{16,20},{18,... | collective-permute-start | bytes 2457608 | tf_op jit(solution)/shard_map/ppermute | solution.py:81
  226.1 25.0 %collective-permute-start.27 = (bf16[2,160,1280]{2,1,0:T(8,128)(2,1)}, bf16[2,160,1280]{2,1,0:T(8,128)(2,1)}, u32[]{:S(2)}, u32[]{:S(2)}) collective-permute-start(bf16[2,160,1280]{2,1,0:T(8,128)(2,1)} %collective-permute-done.26.refs_5_.refs_4_), channel_id=1, source_target_pairs={{0,2},{2,0},{4,6},{6,4},{8,10},{10,8},{12,14},{14,12},{16,18},{18,... | collective-permute-start | bytes 2457608 | tf_op jit(solution)/shard_map/ppermute | solution.py:81
  226.6 111.8 %collective-permute-start.47 = (bf16[256,1280]{1,0:T(8,128)(2,1)}, bf16[256,1280]{1,0:T(8,128)(2,1)}, u32[]{:S(2)}, u32[]{:S(2)}) collective-permute-start(bf16[256,1280]{1,0:T(8,128)(2,1)} %get-tuple-element.145.refs_4_), channel_id=1, source_target_pairs={{0,2},{2,0},{4,6},{6,4},{8,10},{10,8},{12,14},{14,12},{16,18},{18,... | collective-permute-start | bytes 1966088 | tf_op jit(solution)/shard_map/ppermute | solution.py:81
  251.1 23.1 %collective-permute-start.25 = (bf16[256,1280]{1,0:T(8,128)(2,1)}, bf16[256,1280]{1,0:T(8,128)(2,1)}, u32[]{:S(2)}, u32[]{:S(2)}) collective-permute-start(bf16[256,1280]{1,0:T(8,128)(2,1)} %get-tuple-element.149.refs_4_), channel_id=1, source_target_pairs={{0,8},{2,10},{4,12},{6,14},{8,0},{10,2},{12,4},{14,6},{16,24},{18,... | collective-permute-start | bytes 1966088 | tf_op jit(solution)/shard_map/ppermute | solution.py:81
  278.7 38.3 %collective-permute-start.36 = (bf16[2560,256]{1,0:T(8,128)(2,1)}, bf16[2560,256]{1,0:T(8,128)(2,1)}, u32[]{:S(2)}, u32[]{:S(2)}) collective-permute-start(bf16[2560,256]{1,0:T(8,128)(2,1)} %get-tuple-element.163), channel_id=1, source_target_pairs={{0,8},{2,10},{4,12},{6,14},{8,0},{10,2},{12,4},{14,6},{16,24},{18,... | collective-permute-start | bytes 3932168 | tf_op jit(solution)/shard_map/ppermute | solution.py:81
  283.8 32.6 %collective-permute-start.35 = (bf16[1,80,2560]{2,1,0:T(8,128)(2,1)S(1)}, bf16[1,80,2560]{2,1,0:T(8,128)(2,1)S(1)}, u32[]{:S(2)}, u32[]{:S(2)}) collective-permute-start(bf16[1,80,2560]{2,1,0:T(8,128)(2,1)S(1)} %constant_dynamic-slice_fusion.19), channel_id=1, source_target_pairs={{0,1},{1,0},{2,3},{3,2},{4,5},{5,4},{6,7},{7,6},{8,9},{9,8},{10,11... | collective-permute-start | bytes 1228808 | tf_op jit(solution)/shard_map/ppermute | solution.py:74
  286.7 30.2 %collective-permute-start.34 = (bf16[1,80,5120]{2,1,0:T(8,128)(2,1)S(1)}, bf16[1,80,5120]{2,1,0:T(8,128)(2,1)S(1)}, u32[]{:S(2)}, u32[]{:S(2)}) collective-permute-start(bf16[1,80,5120]{2,1,0:T(8,128)(2,1)S(1)} %dynamic-slice_bitcast_fusion.4), channel_id=1, source_target_pairs={{0,4},{2,6},{4,0},{6,2},{8,12},{10,14},{12,8},{14,10},{16,20},{18,... | collective-permute-start | bytes 2457608 | tf_op jit(solution)/shard_map/ppermute | solution.py:81
  287.3 29.1 %collective-permute-start.37 = (bf16[640,256]{1,0:T(8,128)(2,1)}, bf16[640,256]{1,0:T(8,128)(2,1)}, u32[]{:S(2)}, u32[]{:S(2)}) collective-permute-start(bf16[640,256]{1,0:T(8,128)(2,1)} %get-tuple-element.165), channel_id=1, source_target_pairs={{0,8},{2,10},{4,12},{6,14},{8,0},{10,2},{12,4},{14,6},{16,24},{18,... | collective-permute-start | bytes 983048 | tf_op jit(solution)/shard_map/ppermute | solution.py:81
  316.3 26.7 %collective-permute-start.43 = (bf16[256,1280]{1,0:T(8,128)(2,1)}, bf16[256,1280]{1,0:T(8,128)(2,1)}, u32[]{:S(2)}, u32[]{:S(2)}) collective-permute-start(bf16[256,1280]{1,0:T(8,128)(2,1)} %get-tuple-element.149.refs_4_), channel_id=1, source_target_pairs={{0,2},{2,0},{4,6},{6,4},{8,10},{10,8},{12,14},{14,12},{16,18},{18,... | collective-permute-start | bytes 1966088 | tf_op jit(solution)/shard_map/ppermute | solution.py:81
  316.4 26.2 %collective-permute-start.48 = (bf16[256,1280]{1,0:T(8,128)(2,1)}, bf16[256,1280]{1,0:T(8,128)(2,1)}, u32[]{:S(2)}, u32[]{:S(2)}) collective-permute-start(bf16[256,1280]{1,0:T(8,128)(2,1)} %collective-permute-done.22.refs_5_), channel_id=1, source_target_pairs={{0,2},{2,0},{4,6},{6,4},{8,10},{10,8},{12,14},{14,12},{16,18},{18,... | collective-permute-start | bytes 1966088 | tf_op jit(solution)/shard_map/ppermute | solution.py:81
  316.9 39.1 %collective-permute-start.41 = (bf16[2560,256]{1,0:T(8,128)(2,1)}, bf16[2560,256]{1,0:T(8,128)(2,1)}, u32[]{:S(2)}, u32[]{:S(2)}) collective-permute-start(bf16[2560,256]{1,0:T(8,128)(2,1)} %get-tuple-element.166.refs_0_), channel_id=1, source_target_pairs={{0,2},{2,0},{4,6},{6,4},{8,10},{10,8},{12,14},{14,12},{16,18},{18,... | collective-permute-start | bytes 3932168 | tf_op jit(solution)/shard_map/ppermute | solution.py:81
  316.9 27.9 %collective-permute-start.44 = (bf16[256,1280]{1,0:T(8,128)(2,1)}, bf16[256,1280]{1,0:T(8,128)(2,1)}, u32[]{:S(2)}, u32[]{:S(2)}) collective-permute-start(bf16[256,1280]{1,0:T(8,128)(2,1)} %collective-permute-done.25.refs_5_), channel_id=1, source_target_pairs={{0,2},{2,0},{4,6},{6,4},{8,10},{10,8},{12,14},{14,12},{16,18},{18,... | collective-permute-start | bytes 1966088 | tf_op jit(solution)/shard_map/ppermute | solution.py:81
  318.5 35.5 %all-to-all-start.2 = ((bf16[16,1,2,8,1280]{4,3,2,1,0:T(8,128)(2,1)}), bf16[16,1,2,8,1280]{4,3,2,1,0:T(8,128)(2,1)}, u32[]{:S(2)}, u32[]{:S(2)}) async-start(bf16[16,1,2,8,1280]{4,3,2,1,0:T(8,128)(2,1)} %bitcast.33), calls=%async_computation.2 | async-start | bytes 1310720 | tf_op jit(solution)/shard_map/all_to_all | solution.py:749
  344.5 24.3 %collective-permute-start.40 = (bf16[1920,256]{1,0:T(8,128)(2,1)}, bf16[1920,256]{1,0:T(8,128)(2,1)}, u32[]{:S(2)}, u32[]{:S(2)}) collective-permute-start(bf16[1920,256]{1,0:T(8,128)(2,1)} %get-tuple-element.177), channel_id=1, source_target_pairs={{0,8},{2,10},{4,12},{6,14},{8,0},{10,2},{12,4},{14,6},{16,24},{18,... | collective-permute-start | bytes 2949128 | tf_op jit(solution)/shard_map/ppermute | solution.py:81
  356.0 35.8 %collective-permute-start.57 = (bf16[256,1280]{1,0:T(8,128)(2,1)}, bf16[256,1280]{1,0:T(8,128)(2,1)}, u32[]{:S(2)}, u32[]{:S(2)}) collective-permute-start(bf16[256,1280]{1,0:T(8,128)(2,1)} %get-tuple-element.192.refs_2_), channel_id=1, source_target_pairs={{0,2},{2,0},{4,6},{6,4},{8,10},{10,8},{12,14},{14,12},{16,18},{18,... | collective-permute-start | bytes 1966088 | tf_op jit(solution)/shard_map/ppermute | solution.py:81
  356.0 36.3 %collective-permute-start.54 = (bf16[256,1280]{1,0:T(8,128)(2,1)}, bf16[256,1280]{1,0:T(8,128)(2,1)}, u32[]{:S(2)}, u32[]{:S(2)}) collective-permute-start(bf16[256,1280]{1,0:T(8,128)(2,1)} %get-tuple-element.144.refs_4_), channel_id=1, source_target_pairs={{0,2},{2,0},{4,6},{6,4},{8,10},{10,8},{12,14},{14,12},{16,18},{18,... | collective-permute-start | bytes 1966088 | tf_op jit(solution)/shard_map/ppermute | solution.py:81
  366.4 26.0 %collective-permute-start.58 = (bf16[1280,256]{1,0:T(8,128)(2,1)}, bf16[1280,256]{1,0:T(8,128)(2,1)}, u32[]{:S(2)}, u32[]{:S(2)}) collective-permute-start(bf16[1280,256]{1,0:T(8,128)(2,1)} %shard_map.231.refs_0_), channel_id=1, source_target_pairs={{0,2},{2,0},{4,6},{6,4},{8,10},{10,8},{12,14},{14,12},{16,18},{18,... | collective-permute-start | bytes 1966088 | tf_op jit(solution)/shard_map/ppermute | solution.py:81
  367.2 28.4 %collective-permute-start.55 = (bf16[256,1280]{1,0:T(8,128)(2,1)}, bf16[256,1280]{1,0:T(8,128)(2,1)}, u32[]{:S(2)}, u32[]{:S(2)}) collective-permute-start(bf16[256,1280]{1,0:T(8,128)(2,1)} %collective-permute-done.21.refs_5_), channel_id=1, source_target_pairs={{0,2},{2,0},{4,6},{6,4},{8,10},{10,8},{12,14},{14,12},{16,18},{18,... | collective-permute-start | bytes 1966088 | tf_op jit(solution)/shard_map/ppermute | solution.py:81
  368.8 28.2 %collective-permute-start.59 = (bf16[256,1280]{1,0:T(8,128)(2,1)}, bf16[256,1280]{1,0:T(8,128)(2,1)}, u32[]{:S(2)}, u32[]{:S(2)}) collective-permute-start(bf16[256,1280]{1,0:T(8,128)(2,1)} %shard_map.225.refs_2_), channel_id=1, source_target_pairs={{0,2},{2,0},{4,6},{6,4},{8,10},{10,8},{12,14},{14,12},{16,18},{18,... | collective-permute-start | bytes 1966088 | tf_op jit(solution)/shard_map/ppermute | solution.py:81
  395.6 30.1 %collective-permute-start.51 = (bf16[2,320,640]{2,1,0:T(8,128)(2,1)}, bf16[2,320,640]{2,1,0:T(8,128)(2,1)S(1)}, u32[]{:S(2)}, u32[]{:S(2)}) collective-permute-start(bf16[2,320,640]{2,1,0:T(8,128)(2,1)} %dynamic-slice_bitcast_fusion.1), channel_id=1, source_target_pairs={{0,1},{1,0},{2,3},{3,2},{4,5},{5,4},{6,7},{7,6},{8,9},{9,8},{10,11... | collective-permute-start | bytes 2457608 | tf_op jit(solution)/shard_map/ppermute | solution.py:74
  397.0 28.7 %collective-permute-start.49 = (bf16[1,80,5120]{2,1,0:T(8,128)(2,1)}, bf16[1,80,5120]{2,1,0:T(8,128)(2,1)S(1)}, u32[]{:S(2)}, u32[]{:S(2)}) collective-permute-start(bf16[1,80,5120]{2,1,0:T(8,128)(2,1)} %dynamic-slice_bitcast_fusion.2), channel_id=1, source_target_pairs={{0,4},{2,6},{4,0},{6,2},{8,12},{10,14},{12,8},{14,10},{16,20},{18,... | collective-permute-start | bytes 2457608 | tf_op jit(solution)/shard_map/ppermute | solution.py:81
  399.3 26.4 %collective-permute-start.50 = (bf16[1,80,2560]{2,1,0:T(8,128)(2,1)}, bf16[1,80,2560]{2,1,0:T(8,128)(2,1)S(1)}, u32[]{:S(2)}, u32[]{:S(2)}) collective-permute-start(bf16[1,80,2560]{2,1,0:T(8,128)(2,1)} %constant_dynamic-slice_fusion.17), channel_id=1, source_target_pairs={{0,1},{1,0},{2,3},{3,2},{4,5},{5,4},{6,7},{7,6},{8,9},{9,8},{10,11... | collective-permute-start | bytes 1228808 | tf_op jit(solution)/shard_map/ppermute | solution.py:74
  409.5 46.2 %collective-permute-start.61 = (bf16[2,320,640]{2,1,0:T(8,128)(2,1)}, bf16[2,320,640]{2,1,0:T(8,128)(2,1)}, u32[]{:S(2)}, u32[]{:S(2)}) collective-permute-start(bf16[2,320,640]{2,1,0:T(8,128)(2,1)} %dynamic-slice_bitcast_fusion), channel_id=1, source_target_pairs={{0,1},{1,0},{2,3},{3,2},{4,5},{5,4},{6,7},{7,6},{8,9},{9,8},{10,11... | collective-permute-start | bytes 2457608 | tf_op jit(solution)/shard_map/ppermute | solution.py:74
  411.0 44.7 %collective-permute-start.62 = (bf16[2,1,80,1280]{3,2,0,1:T(8,128)(2,1)}, bf16[2,1,80,1280]{3,2,0,1:T(8,128)(2,1)}, u32[]{:S(2)}, u32[]{:S(2)}) collective-permute-start(bf16[2,1,80,1280]{3,2,0,1:T(8,128)(2,1)} %constant_dynamic-slice_fusion.15), channel_id=1, source_target_pairs={{0,4},{2,6},{4,0},{6,2},{8,12},{10,14},{12,8},{14,10},{16,20},{18,... | collective-permute-start | bytes 1228808 | tf_op jit(solution)/shard_map/ppermute | solution.py:81
  431.6 24.1 %collective-permute-start.64 = (bf16[1,320,640]{2,1,0:T(8,128)(2,1)}, bf16[1,320,640]{2,1,0:T(8,128)(2,1)}, u32[]{:S(2)}, u32[]{:S(2)}) collective-permute-start(bf16[1,320,640]{2,1,0:T(8,128)(2,1)} %constant_dynamic-slice_fusion.13), channel_id=1, source_target_pairs={{0,4},{2,6},{4,0},{6,2},{8,12},{10,14},{12,8},{14,10},{16,20},{18,... | collective-permute-start | bytes 1228808 | tf_op jit(solution)/shard_map/ppermute | solution.py:81
  436.1 29.5 %collective-permute-start.63 = (bf16[4,1,80,1280]{3,2,1,0:T(8,128)(2,1)}, bf16[4,1,80,1280]{3,2,1,0:T(8,128)(2,1)}, u32[]{:S(2)}, u32[]{:S(2)}) collective-permute-start(bf16[4,1,80,1280]{3,2,1,0:T(8,128)(2,1)} %constant_dynamic-slice_fusion.14), channel_id=1, source_target_pairs={{0,4},{2,6},{4,0},{6,2},{8,12},{10,14},{12,8},{14,10},{16,20},{18,... | collective-permute-start | bytes 2457608 | tf_op jit(solution)/shard_map/ppermute | solution.py:81
  446.3 36.3 %all-to-all-start.3 = ((bf16[16,1,2,8,1280]{4,3,2,1,0:T(8,128)(2,1)}), bf16[16,1,2,8,1280]{4,3,2,1,0:T(8,128)(2,1)}, u32[]{:S(2)}, u32[]{:S(2)}) async-start(bf16[16,1,2,8,1280]{4,3,2,1,0:T(8,128)(2,1)} %bitcast.54), calls=%async_computation.3 | async-start | bytes 1310720 | tf_op jit(solution)/shard_map/all_to_all | solution.py:749
  470.5 37.0 %collective-permute-start.66 = (bf16[1,2,80,2560]{3,2,1,0:T(8,128)(2,1)}, bf16[1,2,80,2560]{3,2,1,0:T(8,128)(2,1)}, u32[]{:S(2)}, u32[]{:S(2)}) collective-permute-start(bf16[1,2,80,2560]{3,2,1,0:T(8,128)(2,1)} %constant_dynamic-slice_fusion.11), channel_id=1, source_target_pairs={{0,16},{2,18},{4,20},{6,22},{8,24},{10,26},{12,28},{14,30},{16,0},... | collective-permute-start | bytes 2457608 | tf_op jit(solution)/shard_map/ppermute | solution.py:81
  474.1 33.5 %collective-permute-start.65 = (bf16[6,2,80,640]{3,2,0,1:T(8,128)(2,1)}, bf16[6,2,80,640]{3,2,0,1:T(8,128)(2,1)}, u32[]{:S(2)}, u32[]{:S(2)}) collective-permute-start(bf16[6,2,80,640]{3,2,0,1:T(8,128)(2,1)} %constant_dynamic-slice_fusion.12), channel_id=1, source_target_pairs={{0,1},{1,0},{2,3},{3,2},{4,5},{5,4},{6,7},{7,6},{8,9},{9,8},{10,11... | collective-permute-start | bytes 3686408 | tf_op jit(solution)/shard_map/ppermute | solution.py:74
  477.6 50.6 %collective-permute-start.75 = (bf16[4,1,80,640]{3,2,1,0:T(8,128)(2,1)}, bf16[4,1,80,640]{3,2,1,0:T(8,128)(2,1)}, u32[]{:S(2)}, u32[]{:S(2)}) collective-permute-start(bf16[4,1,80,640]{3,2,1,0:T(8,128)(2,1)} %constant_dynamic-slice_fusion.7), channel_id=1, source_target_pairs={{0,1},{1,0},{2,3},{3,2},{4,5},{5,4},{6,7},{7,6},{8,9},{9,8},{10,11... | collective-permute-start | bytes 1228808 | tf_op jit(solution)/shard_map/ppermute | solution.py:74
  480.2 41.6 %collective-permute-start.74 = (bf16[2,1,80,640]{3,2,0,1:T(8,128)(2,1)}, bf16[2,1,80,640]{3,2,0,1:T(8,128)(2,1)}, u32[]{:S(2)}, u32[]{:S(2)}) collective-permute-start(bf16[2,1,80,640]{3,2,0,1:T(8,128)(2,1)} %constant_dynamic-slice_fusion.8), channel_id=1, source_target_pairs={{0,1},{1,0},{2,3},{3,2},{4,5},{5,4},{6,7},{7,6},{8,9},{9,8},{10,11... | collective-permute-start | bytes 614408 | tf_op jit(solution)/shard_map/ppermute | solution.py:74
  514.4 25.6 %collective-permute-start.76 = (bf16[6,1,80,640]{3,2,0,1:T(8,128)(2,1)}, bf16[6,1,80,640]{3,2,0,1:T(8,128)(2,1)}, u32[]{:S(2)}, u32[]{:S(2)}) collective-permute-start(bf16[6,1,80,640]{3,2,0,1:T(8,128)(2,1)} %constant_dynamic-slice_fusion.6), channel_id=1, source_target_pairs={{0,4},{2,6},{4,0},{6,2},{8,12},{10,14},{12,8},{14,10},{16,20},{18,... | collective-permute-start | bytes 1843208 | tf_op jit(solution)/shard_map/ppermute | solution.py:81
  516.2 23.8 %collective-permute-start.73 = (bf16[4,2,80,640]{3,2,1,0:T(8,128)(2,1)}, bf16[4,2,80,640]{3,2,1,0:T(8,128)(2,1)}, u32[]{:S(2)}, u32[]{:S(2)}) collective-permute-start(bf16[4,2,80,640]{3,2,1,0:T(8,128)(2,1)} %constant_dynamic-slice_fusion.9), channel_id=1, source_target_pairs={{0,1},{1,0},{2,3},{3,2},{4,5},{5,4},{6,7},{7,6},{8,9},{9,8},{10,11... | collective-permute-start | bytes 2457608 | tf_op jit(solution)/shard_map/ppermute | solution.py:74
  547.1 22.9 %collective-permute-start.80 = (bf16[4,1,80,640]{3,2,1,0:T(8,128)(2,1)S(1)}, bf16[4,1,80,640]{3,2,1,0:T(8,128)(2,1)S(1)}, u32[]{:S(2)}, u32[]{:S(2)}) collective-permute-start(bf16[4,1,80,640]{3,2,1,0:T(8,128)(2,1)S(1)} %fusion.11), channel_id=1, source_target_pairs={{0,16},{2,18},{4,20},{6,22},{8,24},{10,26},{12,28},{14,30},{16,0},... | collective-permute-start | bytes 1228808 | tf_op jit(solution)/shard_map/ppermute | solution.py:81
  (96 other events, 894.0 us)
